TPU v7x, 32 devices: a whole 2x2x4 slice. The times are simulated.
32 devices in a mesh: sx: 4 (over y, x), sz: 8 (over z, core).
Axes of the slice: x: 2, y: 2, z: 4, core: 2. Of those that a mesh axis runs over, the one named last changes fastest.
Arguments:
- right_side: float32 [72, 256, 4096], P('sx', 'sz'), may hold values from -6 to 6
- coupling: bfloat16 [72, 5, 256, 256], P('sx'), may hold values from -0.15625 to 0.15625
- harmonic_offsets: int32 [5], replicated, may hold values from -6 to 6, as said below
- eigen_basis: bfloat16 [256, 256], replicated, may hold values from -0.375 to 0.375
- eigen_inverse: bfloat16 [256, 256], replicated, may hold values from -0.375 to 0.375
- eigen_size: float32 [256], replicated, may hold values from 0.5 to 50
Outputs:
- solution: float32 [72, 256, 4096], P('sx', 'sz')
Inputs may be any that keep to these rules, and one draw needn't show every extreme that they name: `harmonic_offsets`: the offsets are distinct; some offset equals 6 and some equals -6.
All inputs are finite; a program needn't handle non-finite values.
Results may differ from a plain program's by a relative error of at most 0.00065.
The roundings to bfloat16 on the way count: a program that leaves them out, or rounds other values in their place, can miss the bound.
Values may be sent and summed in bfloat16 or wider, within the bound.
No kernel may reach another device: no remote copies, remote signals or barrier semaphores. Data moves between devices by JAX's collectives and lax.ppermute only.
A program may use at most 192 MiB of HBM per device.

v0:
```python
import jax
import jax.numpy as jnp
from jax import lax
from jax.sharding import PartitionSpec as P

KX = 72
KZ = 128
H = 5
OFF = 6
STEPS = 2
R = 32


def extended(value, sides, width):
    for axis, dim in sides:
        peers, length = (lax.axis_size(axis), value.shape[dim])
        up = [(i, (i + 1) % peers) for i in range(peers)]
        down = [(j, i) for i, j in up]
        last = lax.slice_in_dim(value, length - width, length, axis=dim)
        first = lax.slice_in_dim(value, 0, width, axis=dim)
        before = lax.ppermute(last, axis, up)
        after = lax.ppermute(first, axis, down)
        value = jnp.concatenate([before, value, after], axis=dim)
    return value


def wave_table(mode_count, span_count):
    first_mode = lax.axis_index("sx") * mode_count
    first_span = lax.axis_index("sz") * span_count
    modes = first_mode + jnp.arange(mode_count, dtype=jnp.int32)
    spans = first_span + jnp.arange(span_count, dtype=jnp.int32)
    signed_x = jnp.where(modes < KX // 2, modes, modes - KX).astype(jnp.float32) * (4.0 / KX)
    signed_z = jnp.where(spans < KZ // 2, spans, spans - KZ).astype(jnp.float32) * (4.0 / KZ)
    table = 1.0 + signed_x[:, None] ** 2 + signed_z[None, :] ** 2
    return jnp.repeat(table, R, axis=1)


def precondition(residual, eigen_basis, eigen_inverse, eigen_size, wave_square):
    rounded = residual.astype(jnp.bfloat16)
    spectral = jnp.einsum("ij,kjc->kic", eigen_inverse, rounded, preferred_element_type=jnp.float32)
    factor = -1.0 / (eigen_size[None, :, None] + wave_square[:, None, :])
    scaled = (spectral * factor).astype(jnp.bfloat16)
    result = jnp.einsum("ij,kjc->kic", eigen_basis, scaled, preferred_element_type=jnp.float32)
    return result.astype(jnp.bfloat16)


def apply_operator(search, coupling, harmonic_offsets, wave_square):
    mode_count = search.shape[0]
    padded = extended(search, (("sx", 0),), OFF)
    accum = -wave_square[:, None, :] * search.astype(jnp.float32)
    for harmonic in range(H):
        source = lax.dynamic_slice_in_dim(padded, OFF + harmonic_offsets[harmonic], mode_count, 0)
        accum = accum + jnp.einsum(
            "kij,kjc->kic", coupling[:, harmonic], source, preferred_element_type=jnp.float32
        )
    return accum


def relax(solution, residual, search_full, image):
    inner = jnp.sum(jnp.sum(image * residual, axis=(0, 1)).reshape(-1, R), axis=0)
    energy = jnp.sum(jnp.sum(image * image, axis=(0, 1)).reshape(-1, R), axis=0)
    aligned, total_energy = lax.psum((inner, energy), ("sx", "sz"))
    step_size = jnp.tile(aligned / (total_energy + 1e-06), image.shape[2] // R)
    return (solution + step_size * search_full, residual - step_size * image)


def shards(right_side, coupling, harmonic_offsets, eigen_basis, eigen_inverse, eigen_size):
    residual = lax.all_to_all(right_side, "sz", split_axis=2, concat_axis=1, tiled=True)
    wave_square = wave_table(residual.shape[0], residual.shape[2] // R)
    solution = jnp.zeros_like(residual)
    for sweep in range(STEPS):
        search = precondition(residual, eigen_basis, eigen_inverse, eigen_size, wave_square)
        image = apply_operator(search, coupling, harmonic_offsets, wave_square)
        solution, residual = relax(solution, residual, search.astype(jnp.float32), image)
    return lax.all_to_all(solution, "sz", split_axis=1, concat_axis=2, tiled=True)


def solution(mesh):
    in_specs = (P("sx", "sz", None), P("sx", None, None, None), P(), P(), P(), P())
    out_specs = P("sx", "sz", None)
    return jax.shard_map(shards, mesh=mesh, in_specs=in_specs, out_specs=out_specs, check_vma=False)
```

profile of v0, /device:TPU:0, one launch (start us, length us, event | category | flops | bytes accessed | tf_op | source)
XLA Modules:
  0.0 1065.4 jit_solution(9925449108182842333)
XLA Ops:
  0.0 28.8 %copy.68 = f32[18,32,4096]{1,0,2:T(8,128)} copy(f32[18,32,4096]{2,1,0:T(8,128)} %param.6) | data formatting | bytes 18874368 | tf_op args[0]
  28.8 49.0 %reshape.75 = f32[8,1,294912]{2,1,0:T(1,128)} reshape(f32[4096,18,32]{2,1,0:T(8,128)} %bitcast.115) | data formatting | bytes 18874368
  77.8 6.3 all-to-all-start
  84.4 206.1 %all-to-all-done = f32[8,1,294912]{2,1,0:T(1,128)} async-done(((f32[8,1,294912]{2,1,0:T(1,128)}), f32[8,1,294912]{2,1,0:T(1,128)}, u32[]{:S(2)}, u32[]{:S(2)}) %all-to-all-start) | async-done | bytes 9437216 | tf_op jit(solution)/shard_map/all_to_all | solution.py:68
  291.1 28.4 %reduce = f32[8,294912]{1,0:T(8,128)} reduce(f32[8,1,294912]{2,1,0:T(1,128)} %all-to-all-done, f32[]{:T(128)} %broadcast.95), dimensions={1}, to_apply=%all_to_all.26.reduce_sub_computation | reduce | bytes 18874372 | tf_op jit(solution)/shard_map/all_to_all | solution.py:68
  319.5 44.3 %reshape.76 = f32[4096,18,32]{2,1,0:T(8,128)} reshape(f32[8,294912]{1,0:T(8,128)} %reduce) | data formatting | bytes 18874368
  363.8 31.4 %copy.70 = f32[18,8,32,512]{3,2,1,0:T(8,128)} copy(f32[18,8,32,512]{2,0,3,1:T(8,128)} %bitcast.114) | data formatting | bytes 18874368 | tf_op jit(solution)/shard_map/all_to_all | solution.py:68
  395.2 7.7 copy.71
  402.9 6.3 convert_bitcast_fusion.1
  423.7 27.9 %collective-permute-done = bf16[6,256,512]{2,1,0:T(8,128)(2,1)} collective-permute-done((bf16[6,256,512]{2,1,0:T(8,128)(2,1)}, bf16[6,256,512]{2,1,0:T(8,128)(2,1)}, u32[]{:S(2)}, u32[]{:S(2)}) %collective-permute-start) | collective-permute-done | bytes 1572896 | tf_op jit(solution)/shard_map/ppermute | solution.py:21
  451.7 32.5 %collective-permute-done.1 = bf16[6,256,512]{2,1,0:T(8,128)(2,1)} collective-permute-done((bf16[6,256,512]{2,1,0:T(8,128)(2,1)}, bf16[6,256,512]{2,1,0:T(8,128)(2,1)}, u32[]{:S(2)}, u32[]{:S(2)}) %collective-permute-start.1) | collective-permute-done | bytes 1572896 | tf_op jit(solution)/shard_map/ppermute | solution.py:22
  484.1 4.3 pad_maximum_fusion
  488.5 5.4 fusion.27
  494.0 5.0 fusion.29
  499.0 5.0 fusion.31
  504.0 5.1 fusion.33
  509.1 23.6 %multiply_reduce_fusion.2 = (f32[512]{0:T(512)S(1)}, f32[512]{0:T(512)S(1)}, f32[18,256,512]{2,1,0:T(8,128)}) fusion(f32[18,8,32,512]{3,2,1,0:T(8,128)} %copy.70, bf16[30,256,512]{2,1,0:T(8,128)(2,1)} %copy-done.2, s32[]{:T(128)S(6)} %select_n.42, bf16[18,5,256,256]{3,2,1,0:T(8,128)(2,1)} %param.7, f32[18,512,256]{1,2,0:T(8,128)} %fusion.27, ...), kind=kOutput, calls=%fused_computation.22 | convolution fusion | flops 1233910784 | bytes 68472832 | tf_op jit(solution)/shard_map/kij,kjc->kic/dot_general | solution.py:53
  532.9 37.0 %all-reduce.1 = (f32[32]{0:T(128)S(1)}, f32[32]{0:T(128)S(1)}) all-reduce(f32[32]{0:T(128)S(1)} %reduce_sum.73, f32[32]{0:T(128)S(1)} %reduce_sum.75), channel_id=1, replica_groups=mesh['sx'=4,'sz'=8] {'sx','sz'}, use_global_device_ids=true, to_apply=%region_2.3 | all-reduce | flops 64 | bytes 512 | tf_op jit(solution)/shard_map/psum | solution.py:62
  570.0 9.9 convert_bitcast_fusion
  585.6 35.2 %collective-permute-done.2 = bf16[6,256,512]{2,1,0:T(8,128)(2,1)S(1)} collective-permute-done((bf16[6,256,512]{2,1,0:T(8,128)(2,1)S(1)}, bf16[6,256,512]{2,1,0:T(8,128)(2,1)S(1)}, u32[]{:S(2)}, u32[]{:S(2)}) %collective-permute-start.2) | collective-permute-done | bytes 1572896 | tf_op jit(solution)/shard_map/ppermute | solution.py:21
  620.8 32.2 %collective-permute-done.3 = bf16[6,256,512]{2,1,0:T(8,128)(2,1)S(1)} collective-permute-done((bf16[6,256,512]{2,1,0:T(8,128)(2,1)S(1)}, bf16[6,256,512]{2,1,0:T(8,128)(2,1)S(1)}, u32[]{:S(2)}, u32[]{:S(2)}) %collective-permute-start.3) | collective-permute-done | bytes 1572896 | tf_op jit(solution)/shard_map/ppermute | solution.py:22
  654.3 10.1 fusion.15
  664.4 5.0 fusion.17
  669.4 5.1 fusion.19
  674.6 5.0 fusion.21
  679.6 22.7 %multiply_reduce_fusion = (f32[512]{0:T(512)S(1)}, f32[512]{0:T(512)S(1)}) fusion(f32[18,256,512]{2,1,0:T(8,128)} %get-tuple-element.22, f32[512]{0:T(512)S(1)} %mul.87, f32[18,8,32,512]{3,2,1,0:T(8,128)} %copy.70, bf16[30,256,512]{2,1,0:T(8,128)(2,1)} %copy-done.1, s32[]{:T(128)S(6)} %select_n.42, bf16[18,5,256,256]{3,2,1,0:T(8,128)(2,1)} %param.7, ...), kind=kOutput, calls=%fused_computation.19 | convolution fusion | flops 1238629376 | bytes 68462592 | tf_op jit(solution)/shard_map/kij,kjc->kic/dot_general | solution.py:53
  702.5 40.7 %all-reduce = (f32[32]{0:T(128)S(1)}, f32[32]{0:T(128)S(1)}) all-reduce(f32[32]{0:T(128)S(1)} %reduce_sum.77, f32[32]{0:T(128)S(1)} %reduce_sum.79), channel_id=1, replica_groups=mesh['sx'=4,'sz'=8] {'sx','sz'}, use_global_device_ids=true, to_apply=%region_8.9 | all-reduce | flops 64 | bytes 512 | tf_op jit(solution)/shard_map/psum | solution.py:62
  743.3 9.3 fusion.5
  752.6 9.3 copy.80
  761.9 278.2 %all_to_all.36 = f32[18,256,512]{2,0,1:T(8,128)} all-to-all(f32[18,256,512]{2,0,1:T(8,128)S(1)} %copy.80), channel_id=1, replica_groups=mesh['sx'=4,'sz'=8] {'sz'}, dimensions={1} | all-to-all | bytes 18874368 | tf_op jit(solution)/shard_map/all_to_all | solution.py:75
  1040.1 13.6 %copy.81 = f32[18,32,8,512]{3,2,1,0:T(8,128)} copy(f32[18,32,8,512]{3,0,1,2:T(8,128)} %bitcast.118) | data formatting | bytes 18874368 | tf_op jit(solution)/shard_map/all_to_all | solution.py:75
  1053.7 11.2 %all_to_all.33 = f32[18,32,4096]{2,1,0:T(8,128)} reshape(f32[18,32,8,512]{3,2,1,0:T(8,128)} %copy.81) | data formatting | bytes 18874368 | tf_op jit(solution)/shard_map/all_to_all | solution.py:75
  (65 shorter events, 17.1 us)
Async XLA Ops:
  0.0 402.9 %copy-start = (bf16[256,256]{1,0:T(8,128)(2,1)S(1)}, bf16[256,256]{1,0:T(8,128)(2,1)}, u32[]{:S(2)}) copy-start(bf16[256,256]{1,0:T(8,128)(2,1)} %param.9) | copy-start | bytes 393220
  77.8 212.8 %all-to-all-start = ((f32[8,1,294912]{2,1,0:T(1,128)}), f32[8,1,294912]{2,1,0:T(1,128)}, u32[]{:S(2)}, u32[]{:S(2)}) async-start(f32[8,1,294912]{2,1,0:T(1,128)} %reshape.75), calls=%async_computation | async-start | bytes 18874368 | tf_op jit(solution)/shard_map/all_to_all | solution.py:68
  84.4 318.5 %copy-start.5 = (f32[18,512]{1,0:T(8,128)}, f32[18,512]{1,0:T(8,128)S(1)}, u32[]{:S(2)}) copy-start(f32[18,512]{1,0:T(8,128)S(1)} %broadcast_in_dim_reshape.2) | copy-start | bytes 110596
  395.2 7.7 copy-start.8
  395.2 7.7 copy-start.10
  402.9 13.2 %copy-start.7 = (s32[5]{0:T(128)S(1)}, s32[5]{0:T(128)}, u32[]{:S(2)}) copy-start(s32[5]{0:T(128)} %param.8) | copy-start | bytes 64
  409.3 79.2 %slice-start = ((s8[11796480]{0:T(1024)(128)(4,1)}), s8[3407872]{0:T(1024)(128)(4,1)S(1)}, s32[]{:S(2)}) async-start(s8[11796480]{0:T(1024)(128)(4,1)} %bitcast.119), calls=%async_computation.2 | async-start | bytes 6815744
  413.2 38.5 %collective-permute-start = (bf16[6,256,512]{2,1,0:T(8,128)(2,1)}, bf16[6,256,512]{2,1,0:T(8,128)(2,1)}, u32[]{:S(2)}, u32[]{:S(2)}) collective-permute-start(bf16[6,256,512]{2,1,0:T(8,128)(2,1)} %get-tuple-element.15), channel_id=1, source_target_pairs={{0,8},{8,16},{16,24},{24,0},{1,9},{9,17},{17,25},{25,1},{2,10},{10... | collective-permute-start | bytes 4718600 | tf_op jit(solution)/shard_map/ppermute | solution.py:21
  414.7 69.4 %collective-permute-start.1 = (bf16[6,256,512]{2,1,0:T(8,128)(2,1)}, bf16[6,256,512]{2,1,0:T(8,128)(2,1)}, u32[]{:S(2)}, u32[]{:S(2)}) collective-permute-start(bf16[6,256,512]{2,1,0:T(8,128)(2,1)} %get-tuple-element.16), channel_id=1, source_target_pairs={{8,0},{16,8},{24,16},{0,24},{9,1},{17,9},{25,17},{1,25},{10,2},{18... | collective-permute-start | bytes 4718600 | tf_op jit(solution)/shard_map/ppermute | solution.py:22
  423.7 64.7 %slice-start.1 = ((s8[11796480]{0:T(1024)(128)(4,1)}), s8[4194304]{0:T(1024)(128)(4,1)S(1)}, s32[]{:S(2)}) async-start(s8[11796480]{0:T(1024)(128)(4,1)} %bitcast.119), calls=%async_computation.3 | async-start | bytes 8388608
  423.7 64.7 %slice-start.2 = ((s8[11796480]{0:T(1024)(128)(4,1)}), s8[4194304]{0:T(1024)(128)(4,1)S(1)}, s32[]{:S(2)}) async-start(s8[11796480]{0:T(1024)(128)(4,1)} %bitcast.119), calls=%async_computation.4 | async-start | bytes 8388608
  488.5 15.5 %copy-start.2 = (bf16[30,256,512]{2,1,0:T(8,128)(2,1)}, bf16[30,256,512]{2,1,0:T(8,128)(2,1)S(1)}, u32[]{:S(2)}) copy-start(bf16[30,256,512]{2,1,0:T(8,128)(2,1)S(1)} %pad_maximum_fusion) | copy-start | bytes 23592964
  509.1 60.9 %copy-start.6 = (f32[18,512]{1,0:T(8,128)S(1)}, f32[18,512]{1,0:T(8,128)}, u32[]{:S(2)}) copy-start(f32[18,512]{1,0:T(8,128)} %copy-done.5) | copy-start | bytes 110596
  509.1 60.9 %copy-start.9 = (bf16[256,256]{1,0:T(8,128)(2,1)S(1)}, bf16[256,256]{1,0:T(8,128)(2,1)}, u32[]{:S(2)}) copy-start(bf16[256,256]{1,0:T(8,128)(2,1)} %param.10) | copy-start | bytes 393220
  580.0 73.1 %copy-start.3 = (bf16[18,256,512]{2,1,0:T(8,128)(2,1)S(1)}, bf16[18,256,512]{2,1,0:T(8,128)(2,1)}, u32[]{:S(2)}) copy-start(bf16[18,256,512]{2,1,0:T(8,128)(2,1)} %convert_bitcast_fusion) | copy-start | bytes 14155780
  582.2 38.6 %collective-permute-start.2 = (bf16[6,256,512]{2,1,0:T(8,128)(2,1)S(1)}, bf16[6,256,512]{2,1,0:T(8,128)(2,1)S(1)}, u32[]{:S(2)}, u32[]{:S(2)}) collective-permute-start(bf16[6,256,512]{2,1,0:T(8,128)(2,1)S(1)} %get-tuple-element.13), channel_id=1, source_target_pairs={{0,8},{8,16},{16,24},{24,0},{1,9},{9,17},{17,25},{25,1},{2,10},{10... | collective-permute-start | bytes 4718600 | tf_op jit(solution)/shard_map/ppermute | solution.py:21
  584.6 68.5 %collective-permute-start.3 = (bf16[6,256,512]{2,1,0:T(8,128)(2,1)S(1)}, bf16[6,256,512]{2,1,0:T(8,128)(2,1)S(1)}, u32[]{:S(2)}, u32[]{:S(2)}) collective-permute-start(bf16[6,256,512]{2,1,0:T(8,128)(2,1)S(1)} %get-tuple-element.14), channel_id=1, source_target_pairs={{8,0},{16,8},{24,16},{0,24},{9,1},{17,9},{25,17},{1,25},{10,2},{18... | collective-permute-start | bytes 4718600 | tf_op jit(solution)/shard_map/ppermute | solution.py:22
  653.1 11.3 %slice-start.3 = ((s8[11796480]{0:T(1024)(128)(4,1)}), s8[4194304]{0:T(1024)(128)(4,1)S(1)}, s32[]{:S(2)}) async-start(s8[11796480]{0:T(1024)(128)(4,1)} %bitcast.121), calls=%async_computation.5 | async-start | bytes 8388608
  653.1 11.3 %slice-start.4 = ((s8[11796480]{0:T(1024)(128)(4,1)}), s8[4194304]{0:T(1024)(128)(4,1)S(1)}, s32[]{:S(2)}) async-start(s8[11796480]{0:T(1024)(128)(4,1)} %bitcast.121), calls=%async_computation.6 | async-start | bytes 8388608
  654.3 20.3 %copy-start.1 = (bf16[30,256,512]{2,1,0:T(8,128)(2,1)}, bf16[30,256,512]{2,1,0:T(8,128)(2,1)S(1)}, u32[]{:S(2)}) copy-start(bf16[30,256,512]{2,1,0:T(8,128)(2,1)S(1)} %pad_maximum_fusion.1) | copy-start | bytes 23592964
  654.3 10.1 slice-start.5
  674.6 5.0 copy-start.4
where the time goes:
time: 1070 us
  blocking collectives  356 us (33%)
  waiting for transfers between devices  334 us (31%)
  local copies, waits for them, and re-layouts  203 us (19%)
  matrix products  108 us (10%)
  other arithmetic  44.8 us (4%)
  starting transfers between devices  12.6 us (1%)
    all_to_all x1, blocking collectives, shards(): lax.all_to_all(solution, 'sz', split_axis=1, concat_axis=2, tiled=True)  278 us
    all_to_all x1, waiting for transfers between devices, shards(): lax.all_to_all(right_side, 'sz', split_axis=2, concat_axis=1, tiled=True)  206 us
    unnamed x37, local copies, waits for them, and re-layouts  122 us
    dot_general x10, matrix products, apply_operator(): jnp.einsum('kij,kjc->kic', coupling[:, harmonic], source, preferred_eleme...  92.2 us
    psum x2, blocking collectives, relax(): aligned, total_energy = lax.psum((inner, energy), ('sx', 'sz'))  77.7 us
    ppermute x2, waiting for transfers between devices, extended(): after = lax.ppermute(first, axis, down)  64.7 us
    ppermute x2, waiting for transfers between devices, extended(): before = lax.ppermute(last, axis, up)  63.2 us
    all_to_all x3, local copies, waits for them, and re-layouts, shards(): lax.all_to_all(right_side, 'sz', split_axis=2, concat_axis=1, tiled=True)  39.6 us
  transfers between devices with their start and end apart: 5, of which 5 were waited for; matrix products, arithmetic and copies ran while one was open for 0% of the time, Pallas kernels for 0%

commit v1 on v0

v1 whole, which is shorter than its diff:
```python
import functools
import jax
import jax.numpy as jnp
from jax import lax
from jax.experimental import pallas as pl
from jax.experimental.pallas import tpu as pltpu
from jax.sharding import PartitionSpec as P

KX = 72
KZ = 128
H = 5
OFF = 6
R = 32
CHUNKS = ((0, 16), (16, 16))
F32 = jnp.float32
BF16 = jnp.bfloat16
TOP = 2.0**14
UNIT = 2.0**23
STEP = 3
VMEM = 24 * 2**20


class Order:
    def __init__(self):
        self.token = jnp.zeros((8, 128), F32)


def call(order, body, grid, in_specs, out_specs, out_shape, flops, moved, scratch=(), scalars=0):
    outs = len(out_shape)
    inputs = len(in_specs)

    def ordered(*refs):
        before, held, rest = refs[:scalars], refs[scalars : scalars + inputs], refs[scalars + inputs + 1 :]
        rest[outs][...] = jnp.zeros((8, 128), F32)
        body(*before, *held, *rest[:outs], *rest[outs + 1 :])

    kernel = pl.pallas_call(
        ordered,
        grid_spec=pltpu.PrefetchScalarGridSpec(
            num_scalar_prefetch=scalars,
            grid=grid,
            in_specs=in_specs + [pl.BlockSpec(memory_space=pl.ANY)],
            out_specs=out_specs + [whole((8, 128))],
            scratch_shapes=list(scratch),
        ),
        out_shape=out_shape + [jax.ShapeDtypeStruct((8, 128), F32)],
        compiler_params=pltpu.CompilerParams(vmem_limit_bytes=VMEM),
        cost_estimate=pl.CostEstimate(flops=int(flops), bytes_accessed=int(moved), transcendentals=0),
    )

    def run(*args):
        *given, order.token = kernel(*args, order.token)
        return given if outs > 1 else given[0]

    return run


def whole(shape):
    return pl.BlockSpec(shape, lambda m, *_: (0,) * len(shape))


def by_mode(shape, axis=0):
    return pl.BlockSpec(shape, lambda m, *_: (0,) * axis + (m,) + (0,) * (len(shape) - axis - 1))


def dot(a, b):
    return jnp.dot(a, b, preferred_element_type=F32)


def pack_body(parts, x_ref, *refs):
    picks, outs = refs[: len(parts)], refs[len(parts) :]
    modes, rows, columns = x_ref.shape
    width = picks[0].shape[0]
    peers = columns // width
    blocks = [x_ref[m, :, p * width : (p + 1) * width] for p in range(peers) for m in range(modes)]
    value = jnp.concatenate(blocks, axis=0)
    high = value.astype(BF16)
    if any(parts):
        wide = high.astype(F32)
        ratio = (value - wide) / jnp.where(wide == 0.0, 1.0, wide)
        code = jnp.clip(jnp.round(ratio * UNIT), -32767.0, 32767.0)
        upper = jnp.round(code * (1.0 / 256.0))
        lower = (code - upper * 256.0).astype(BF16)
        upper = upper.astype(BF16)
    for part, pick_ref, out_ref in zip(parts, picks, outs):
        if part:
            moved = dot(upper, pick_ref[...]) * 256.0 + dot(lower, pick_ref[...])
            moved = moved.astype(jnp.int32).astype(jnp.int16)
        else:
            moved = dot(high, pick_ref[...]).astype(BF16)
        for peer in range(peers):
            for mode in range(modes):
                at = (peer * modes + mode) * rows
                out_ref[peer, mode] = moved[at : at + rows]


def pack(order, right_side, picks, parts, peers):
    count, rows, columns = right_side.shape
    outs = [(peers, STEP, rows, pick.shape[1]) for pick in picks]
    kinds = [jnp.int16 if part else BF16 for part in parts]
    made = call(
        order,
        functools.partial(pack_body, parts),
        (count // STEP,),
        [by_mode((STEP, rows, columns))] + [whole(pick.shape) for pick in picks],
        [by_mode(shape, 1) for shape in outs],
        [jax.ShapeDtypeStruct((p, count, r, w), kind) for (p, _, r, w), kind in zip(outs, kinds)],
        2 * count * rows * columns * sum(pick.shape[1] * (1 + part) for pick, part in zip(picks, parts)),
        count * rows * columns * 4 + sum(2 * peers * count * rows * pick.shape[1] for pick in picks),
    )(right_side, *picks)
    return made if len(parts) > 1 else [made]


def pick_matrix(spans, first, amount):
    source = jnp.arange(spans * R, dtype=jnp.int32)[:, None]
    target = jnp.arange(spans * amount, dtype=jnp.int32)[None, :]
    wanted = (target // amount) * R + first + target % amount
    return (source == wanted).astype(BF16)


def gate_body(value_ref, token_ref, out_ref, next_ref):
    next_ref[...] = jnp.zeros((8, 128), F32)


def gate(order, value):
    far = pl.BlockSpec(memory_space=pl.ANY)
    value, order.token = pl.pallas_call(
        gate_body,
        in_specs=[far, far],
        out_specs=[far, pl.BlockSpec(memory_space=pltpu.VMEM)],
        out_shape=[jax.ShapeDtypeStruct(value.shape, value.dtype), jax.ShapeDtypeStruct((8, 128), F32)],
        input_output_aliases={0: 0},
    )(value, order.token)
    return value


def fold(payload, amount):
    width = payload.shape[1]
    row = lax.broadcasted_iota(jnp.int32, (width, width), 0)
    column = lax.broadcasted_iota(jnp.int32, (width, width), 1)
    same = ((row & (amount - 1)) == (column & (amount - 1))).astype(F32).astype(BF16)
    high = payload.astype(BF16)
    payload = payload - high.astype(F32)
    middle = payload.astype(BF16)
    low = (payload - middle.astype(F32)).astype(BF16)
    return dot(high, same) + (dot(middle, same) + dot(low, same))


def step_size(total):
    return total[0:1] / (total[1:2] + 1e-06)


def ceiling(first_total, second_total):
    reach = jnp.abs(step_size(first_total)) * jnp.sqrt(first_total[2:3])
    reach = reach + jnp.abs(step_size(second_total)) * jnp.sqrt(second_total[2:3])
    return jnp.maximum(jnp.max(reach, axis=1, keepdims=True), 1e-30)


def fold_rows(value):
    return jnp.sum(value.reshape(-1, 8, value.shape[-1]), axis=0)


def column_sum(value):
    return jnp.sum(value, axis=0, keepdims=True)


def is_first():
    return pl.program_id(0) == 0


def is_last():
    return pl.program_id(0) == pl.num_programs(0) - 1


def zero(ref):
    @pl.when(is_first())
    def _():
        ref[...] = jnp.zeros_like(ref)


def direction(rounded, wave, inverse_ref, basis_ref, size_ref):
    spectral = dot(inverse_ref[...], rounded)
    scaled = (spectral * (-1.0 / (size_ref[...] + wave))).astype(BF16)
    return dot(basis_ref[...], scaled).astype(BF16)


def hand_out(searches, search_ref, first_ref, last_ref, norm_ref, norm_scratch):
    at = pl.program_id(0)
    edge = OFF // STEP
    zero(norm_scratch)
    for i, search in enumerate(searches):
        search_ref[i] = search
        wide = search.astype(F32)
        norm_scratch[...] += fold_rows(wide * wide)

    @pl.when(at < edge)
    def _():
        for i, search in enumerate(searches):
            first_ref[i] = search

    @pl.when(at >= pl.num_programs(0) - edge)
    def _():
        for i, search in enumerate(searches):
            last_ref[i] = search

    @pl.when(is_last())
    def _():
        norm_ref[...] = norm_scratch[...]


def begin_body(high_ref, inverse_ref, basis_ref, size_ref, wave_ref, *outs):
    points = inverse_ref.shape[0]
    searches = []
    for i in range(STEP):
        rounded = high_ref[:, i].reshape(points, -1)
        searches.append(direction(rounded, wave_ref[i], inverse_ref, basis_ref, size_ref))
    hand_out(searches, *outs)


def edge_specs(count, points, width):
    shape = (STEP, points, width)
    edge = OFF // STEP
    first = pl.BlockSpec(shape, lambda m, *_: (jnp.minimum(m, edge - 1), 0, 0))
    last = pl.BlockSpec(shape, lambda m, *_: (jnp.maximum(m - (count // STEP - edge), 0), 0, 0))
    return [by_mode(shape), first, last, whole((8, width))]


def edge_shapes(count, points, width):
    shapes = [(count, points, width), (OFF, points, width), (OFF, points, width)]
    return [jax.ShapeDtypeStruct(s, BF16) for s in shapes] + [jax.ShapeDtypeStruct((8, width), F32)]


def begin(order, high, inverse, basis, size, wave):
    peers, count, rows, width = high.shape
    points = peers * rows
    return call(
        order,
        begin_body,
        (count // STEP,),
        [by_mode((peers, STEP, rows, width), 1), whole(inverse.shape), whole(basis.shape), whole(size.shape), by_mode((STEP, 1, width))],
        edge_specs(count, points, width),
        edge_shapes(count, points, width),
        4 * count * points * points * width,
        4 * count * points * width,
        scratch=[pltpu.VMEM((8, width), F32)],
    )(high, inverse, basis, size, wave)


def removed(high_ref, low_ref, i):
    high = high_ref[:, i].astype(F32)
    return (high * (1.0 / UNIT)) * low_ref[:, i].astype(jnp.int32).astype(F32)


def again_body(amount, high_ref, low_ref, image_ref, total_ref, inverse_ref, basis_ref, size_ref, wave_ref, residual_ref, *rest):
    outs, step_ref = rest[:-1], rest[-1]
    points = inverse_ref.shape[0]

    @pl.when(is_first())
    def _():
        step_ref[0:1] = step_size(fold(total_ref[...], amount))

    searches = []
    for i in range(STEP):
        held = high_ref[:, i].astype(F32) + removed(high_ref, low_ref, i)
        residual = held.reshape(points, -1) - step_ref[0:1] * image_ref[i]
        residual_ref[i] = residual
        searches.append(direction(residual.astype(BF16), wave_ref[i], inverse_ref, basis_ref, size_ref))
    hand_out(searches, *outs)


def again(order, amount, high, low, image, total, inverse, basis, size, wave):
    peers, count, rows, width = high.shape
    points = peers * rows
    block = by_mode((peers, STEP, rows, width), 1)
    plane = by_mode((STEP, points, width))
    return call(
        order,
        functools.partial(again_body, amount),
        (count // STEP,),
        [block, block, plane, whole(total.shape), whole(inverse.shape), whole(basis.shape), whole(size.shape), by_mode((STEP, 1, width))],
        [plane] + edge_specs(count, points, width),
        [jax.ShapeDtypeStruct((count, points, width), F32)] + edge_shapes(count, points, width),
        4 * count * points * points * width,
        14 * count * points * width,
        scratch=[pltpu.VMEM((8, width), F32), pltpu.VMEM((8, width), F32)],
    )(high, low, image, total, inverse, basis, size, wave)


def bring(before_ref, search_ref, after_ref, padded_ref, arrived):
    count = search_ref.shape[0]

    @pl.when(is_first())
    def _():
        parts = [
            pltpu.make_async_copy(before_ref, padded_ref.at[pl.ds(0, OFF)], arrived.at[0]),
            pltpu.make_async_copy(search_ref, padded_ref.at[pl.ds(OFF, count)], arrived.at[1]),
            pltpu.make_async_copy(after_ref, padded_ref.at[pl.ds(OFF + count, OFF)], arrived.at[2]),
        ]
        for part in parts:
            part.start()
        for part in parts:
            part.wait()


def operate(i, offsets_ref, coupling_ref, wave_ref, padded_ref):
    mode = pl.program_id(0) * STEP + i
    blocks = jnp.concatenate([coupling_ref[i, h] for h in range(H)], axis=1)
    sources = jnp.concatenate([padded_ref[mode + OFF + offsets_ref[h]] for h in range(H)], axis=0)
    return dot(blocks, sources) - wave_ref[i] * padded_ref[mode + OFF].astype(F32)


def apply_body(offsets_ref, before_ref, search_ref, after_ref, coupling_ref, wave_ref, high_ref, image_ref, sums_ref, padded_ref, arrived, sums):
    bring(before_ref, search_ref, after_ref, padded_ref, arrived)
    zero(sums)
    for i in range(STEP):
        image = operate(i, offsets_ref, coupling_ref, wave_ref, padded_ref)
        image_ref[i] = image
        sums[0:8] += fold_rows(image * high_ref[:, i].reshape(image.shape).astype(F32))
        sums[8:16] += fold_rows(image * image)

    @pl.when(is_last())
    def _():
        sums_ref[...] = jnp.zeros_like(sums_ref)
        sums_ref[0:1] = column_sum(sums[0:8])
        sums_ref[1:2] = column_sum(sums[8:16])


def apply_last_body(offsets_ref, before_ref, search_ref, after_ref, coupling_ref, wave_ref, residual_ref, norm_ref, sums_ref, padded_ref, arrived, sums):
    bring(before_ref, search_ref, after_ref, padded_ref, arrived)
    zero(sums)
    for i in range(STEP):
        image = operate(i, offsets_ref, coupling_ref, wave_ref, padded_ref)
        sums[0:8] += fold_rows(image * residual_ref[i])
        sums[8:16] += fold_rows(image * image)

    @pl.when(is_last())
    def _():
        sums_ref[...] = jnp.zeros_like(sums_ref)
        sums_ref[0:1] = column_sum(sums[0:8])
        sums_ref[1:2] = column_sum(sums[8:16])
        sums_ref[2:3] = column_sum(norm_ref[...])


def operator_specs(points, width):
    far = pl.BlockSpec(memory_space=pl.ANY)
    return [far, far, far, by_mode((STEP, H, points, points)), by_mode((STEP, 1, width))]


def operator_scratch(count, points, width):
    return [pltpu.VMEM((count + 2 * OFF, points, width), BF16), pltpu.SemaphoreType.DMA((3,)), pltpu.VMEM((16, width), F32)]


def apply(order, offsets, before, search, after, coupling, wave, high):
    count, points, width = search.shape
    peers, _, rows, _ = high.shape
    return call(
        order,
        apply_body,
        (count // STEP,),
        operator_specs(points, width) + [by_mode((peers, STEP, rows, width), 1)],
        [by_mode((STEP, points, width)), whole((8, width))],
        [jax.ShapeDtypeStruct((count, points, width), F32), jax.ShapeDtypeStruct((8, width), F32)],
        2 * H * count * points * points * width,
        2 * count * points * (H * points + 5 * width),
        scratch=operator_scratch(count, points, width),
        scalars=1,
    )(offsets, before, search, after, coupling, wave, high)


def apply_last(order, offsets, before, search, after, coupling, wave, residual, norm):
    count, points, width = search.shape
    return call(
        order,
        apply_last_body,
        (count // STEP,),
        operator_specs(points, width) + [by_mode((STEP, points, width)), whole(norm.shape)],
        [whole((8, width))],
        [jax.ShapeDtypeStruct((8, width), F32)],
        2 * H * count * points * points * width,
        2 * count * points * (H * points + 3 * width),
        scratch=operator_scratch(count, points, width),
        scalars=1,
    )(offsets, before, search, after, coupling, wave, residual, norm)


def rest_body(image_ref, high_ref, low_ref, sums_ref, norm_ref, out_ref, sums):
    zero(sums)
    for i in range(STEP):
        image = image_ref[i]
        sums[...] += fold_rows(image * removed(high_ref, low_ref, i).reshape(image.shape))

    @pl.when(is_last())
    def _():
        out_ref[...] = sums_ref[...]
        out_ref[0:1] += column_sum(sums[...])
        out_ref[2:3] = column_sum(norm_ref[...])


def rest(order, image, high, low, sums, norm):
    count, points, width = image.shape
    peers, _, rows, _ = low.shape
    return call(
        order,
        rest_body,
        (count // STEP,),
        [by_mode((STEP, points, width))] + [by_mode((peers, STEP, rows, width), 1)] * 2 + [whole(sums.shape), whole(norm.shape)],
        [whole((8, width))],
        [jax.ShapeDtypeStruct((8, width), F32)],
        2 * count * points * width,
        8 * count * points * width,
        scratch=[pltpu.VMEM((8, width), F32)],
    )(image, high, low, sums, norm)


def combine_body(amount, one_ref, two_ref, first_ref, second_ref, out_ref, step_ref):
    @pl.when(pl.program_id(0) == 0)
    def _():
        first_total = fold(first_ref[...], amount)
        second_total = fold(second_ref[...], amount)
        step_ref[0:1] = step_size(first_total)
        step_ref[1:2] = step_size(second_total)
        step_ref[2:3] = jnp.broadcast_to(TOP / ceiling(first_total, second_total), (1, step_ref.shape[1]))

    for i in range(STEP):
        value = step_ref[0:1] * one_ref[i].astype(F32) + step_ref[1:2] * two_ref[i].astype(F32)
        out_ref[:, i] = (value * step_ref[2:3]).reshape(out_ref.shape[0], out_ref.shape[2], -1)


def combine(order, amount, one, two, first_total, second_total, peers):
    count, points, width = one.shape
    rows = points // peers
    plane = by_mode((STEP, points, width))
    return call(
        order,
        functools.partial(combine_body, amount),
        (count // STEP,),
        [plane, plane, whole((8, width)), whole((8, width))],
        [by_mode((peers, STEP, rows, width), 1)],
        [jax.ShapeDtypeStruct((peers, count, rows, width), F32)],
        4 * count * points * width,
        8 * count * points * width,
        scratch=[pltpu.VMEM((8, width), F32)],
    )(one, two, first_total, second_total)


def spread_body(*refs):
    amounts = [amount for _, amount in CHUNKS]
    n = len(amounts)
    values, firsts, seconds = refs[:n], refs[n : 2 * n], refs[2 * n : 3 * n]
    place_ref, out_ref, scale_ref = refs[3 * n :]
    peers, modes, rows, _ = values[0].shape
    width = place_ref.shape[1]

    @pl.when(pl.program_id(0) == 0)
    def _():
        side = lax.broadcasted_iota(jnp.int32, (1, width), 1) & (R - 1)
        scale = jnp.zeros((1, width), F32)
        for (first, amount), one_ref, two_ref in zip(CHUNKS, firsts, seconds):
            top = ceiling(fold(one_ref[...], amount), fold(two_ref[...], amount)) * (1.0 / TOP)
            scale = jnp.where((side >= first) & (side < first + amount), top, scale)
        scale_ref[0:1] = scale

    joined = jnp.concatenate([v[...].reshape(peers * modes * rows, v.shape[3]) for v in values], axis=1)
    high = joined.astype(BF16)
    low = (joined - high.astype(F32)).astype(BF16)
    moved = (dot(high, place_ref[...]) + dot(low, place_ref[...])) * scale_ref[0:1]
    for peer in range(peers):
        for mode in range(modes):
            at = (peer * modes + mode) * rows
            out_ref[mode, :, peer * width : (peer + 1) * width] = moved[at : at + rows]


def spread(order, values, firsts, seconds, place):
    peers, count, rows, _ = values[0].shape
    step = STEP
    width = place.shape[1]
    columns = peers * width
    return call(
        order,
        spread_body,
        (count // step,),
        [by_mode((peers, step, rows, v.shape[3]), 1) for v in values]
        + [whole(t.shape) for t in firsts + seconds]
        + [whole(place.shape)],
        [by_mode((step, rows, columns))],
        [jax.ShapeDtypeStruct((count, rows, columns), F32)],
        4 * count * rows * columns * width,
        8 * count * rows * columns,
        scratch=[pltpu.VMEM((8, width), F32)],
    )(*values, *firsts, *seconds, place)


def swap(value):
    return lax.all_to_all(value, "sz", split_axis=0, concat_axis=0, tiled=True)


def edges(first, last):
    peers = lax.axis_size("sx")
    up = [(i, (i + 1) % peers) for i in range(peers)]
    down = [(j, i) for i, j in up]
    return lax.ppermute(last, "sx", up), lax.ppermute(first, "sx", down)


def exchange(value, axis, distance):
    return lax.ppermute(value, axis, [(i, i ^ distance) for i in range(lax.axis_size(axis))])


def total_span(value):
    value = value + exchange(value, "sz", 1)
    return sum([exchange(value, "sz", d) for d in range(2, lax.axis_size("sz"), 2)], value)


def total_mode(value):
    distance = 1
    while distance < lax.axis_size("sx"):
        value = value + exchange(value, "sx", distance)
        distance *= 2
    return value


def wave_table(mode_count, span_count, amount):
    first_mode = lax.axis_index("sx") * mode_count
    first_span = lax.axis_index("sz") * span_count
    modes = first_mode + jnp.arange(mode_count, dtype=jnp.int32)
    spans = first_span + jnp.arange(span_count * amount, dtype=jnp.int32) // amount
    signed_x = jnp.where(modes < KX // 2, modes, modes - KX).astype(F32) * (4.0 / KX)
    signed_z = jnp.where(spans < KZ // 2, spans, spans - KZ).astype(F32) * (4.0 / KZ)
    return 1.0 + signed_x[:, None, None] ** 2 + signed_z[None, None, :] ** 2


class Chunk:
    def __init__(self, order, arrays, first, amount):
        self.order, self.amount = order, amount
        self.right_side, self.coupling, self.offsets, self.basis, self.inverse, self.size = arrays
        self.peers = lax.axis_size("sz")
        self.spans = KZ // self.peers
        self.pick = pick_matrix(self.spans, first, amount)
        self.wave = wave_table(self.right_side.shape[0], self.spans, amount)

    def send_high(self):
        self.high = swap(self.high)

    def send_low(self):
        self.low = swap(self.low)

    def gate_high(self):
        self.high = swap(gate(self.order, self.high))

    def gate_low(self):
        self.low = swap(gate(self.order, self.low))

    def begin(self):
        self.one, first, last, self.norm = begin(self.order, self.high, self.inverse, self.basis, self.size, self.wave)
        self.before, self.after = edges(first, last)

    def apply(self):
        self.image, self.sums = apply(
            self.order, self.offsets, self.before, self.one, self.after, self.coupling, self.wave, self.high
        )

    def rest(self):
        spans = total_span(rest(self.order, self.image, self.high, self.low, self.sums, self.norm))
        self.order.token = spans
        self.first = total_mode(spans)

    def again(self):
        self.residual, self.two, first, last, self.norm = again(
            self.order, self.amount, self.high, self.low, self.image, self.first, self.inverse, self.basis, self.size, self.wave
        )
        self.before, self.after = edges(first, last)

    def finish(self):
        sums = apply_last(
            self.order, self.offsets, self.before, self.two, self.after, self.coupling, self.wave, self.residual, self.norm
        )
        self.second = total_mode(total_span(sums))

    def combine(self):
        sent = combine(self.order, self.amount, self.one, self.two, self.first, self.second, self.peers)
        self.value = swap(sent.astype(jnp.float16)).astype(F32)


PLAN = (
    "send_high0 send_low0 begin0 apply0 rest0 gate_high1 again0 gate_low1 begin1 finish0 "
    "apply1 rest1 combine0 again1 finish1 combine1"
)


def shards(right_side, coupling, offsets, basis, inverse, size):
    order = Order()
    arrays = (right_side, coupling, offsets, basis, inverse, size[:, None])
    chunks = [Chunk(order, arrays, first, amount) for first, amount in CHUNKS]
    peers = chunks[0].peers
    chunks[0].high, = pack(order, right_side, [chunks[0].pick], (0,), peers)
    others = [(chunks[0], 1)] + [(chunk, part) for chunk in chunks[1:] for part in (0, 1)]
    made = pack(order, right_side, [chunk.pick for chunk, _ in others], tuple(part for _, part in others), peers)
    for (chunk, part), value in zip(others, made):
        setattr(chunk, "low" if part else "high", value)
    for step in PLAN.split():
        getattr(chunks[int(step[-1])], step[:-1])()
    place = jnp.concatenate([c.pick.T for c in chunks], axis=0)
    return spread(order, [c.value for c in chunks], [c.first for c in chunks], [c.second for c in chunks], place)


def solution(mesh):
    in_specs = (P("sx", "sz", None), P("sx", None, None, None), P(), P(), P(), P())
    out_specs = P("sx", "sz", None)
    return jax.shard_map(shards, mesh=mesh, in_specs=in_specs, out_specs=out_specs, check_vma=False)
```

time: 1070 us -> 466 us (0.44)
  blocking collectives: 356 us -> 0 us
  local copies, waits for them, and re-layouts: 203 us -> 51.9 us
  matrix products: 108 us -> 0 us
  waiting for transfers between devices: 334 us -> 254 us
  Pallas kernels: 0 us -> 78.5 us
  starting transfers between devices: 12.6 us -> 68.1 us
  other arithmetic: 44.8 us -> 11.9 us
    all_to_all x1 -> x0, blocking collectives: 278 us -> none  [shards(): lax.all_to_all(solution, 'sz', split_axis=1, concat_axis=2, tiled=True)]
    dot_general x12 -> x0, matrix products: 108 us -> none  [the longest x10 92.2 us: apply_operator(): jnp.einsum('kij,kjc->kic', coupling[:, harmonic], source, preferred_eleme...]
    all_to_all x1 -> x6, waiting for transfers between devices: 206 us -> 116 us  [swap(): return lax.all_to_all(value, 'sz', split_axis=0, concat_axis=0, tiled=True)]
    pallas_call x0 -> x17, Pallas kernels: none -> 78.5 us  [the longest x15 77.3 us: run(): *given, order.token = kernel(*args, order.token)]
    psum x2 -> x0, blocking collectives: 77.7 us -> none  [relax(): aligned, total_energy = lax.psum((inner, energy), ('sx', 'sz'))]
    unnamed x37 -> x74, local copies, waits for them, and re-layouts: 122 us -> 51.8 us
    all_to_all x5 -> x0, local copies, waits for them, and re-layouts: 64.4 us -> none  [the longest x3 39.6 us: shards(): lax.all_to_all(right_side, 'sz', split_axis=2, concat_axis=1, tiled=True)]
    ppermute x4 -> x32, starting transfers between devices: 6.27 us -> 40 us  [the longest x24 28.1 us: exchange(): lax.ppermute(value, axis, [(i, i ^ distance) for i in range(lax.axis_size...]
  transfers between devices with their start and end apart: 5 -> 38, of which waited for: 5 -> 27; matrix products, arithmetic and copies ran while one was open for 0% -> 1% of each run, Pallas kernels for 0% -> 13%
where the time goes in v1:
time: 466 us; the launch traced here: 465 us
  waiting for transfers between devices  254 us (55%)
  Pallas kernels  78.5 us (17%)
  starting transfers between devices  68.1 us (15%)
  local copies, waits for them, and re-layouts  51.9 us (11%)
  other arithmetic  11.9 us (3%)
    all_to_all x6, waiting for transfers between devices, swap(): return lax.all_to_all(value, 'sz', split_axis=0, concat_axis=0, tiled=True)  116 us
    ppermute x8, waiting for transfers between devices, edges(): return (lax.ppermute(last, 'sx', up), lax.ppermute(first, 'sx', down))  104 us
    pallas_call x15, Pallas kernels, run(): *given, order.token = kernel(*args, order.token)  77.3 us
    unnamed x74, local copies, waits for them, and re-layouts  51.8 us
    ppermute x24, waiting for transfers between devices, exchange(): lax.ppermute(value, axis, [(i, i ^ distance) for i in range(lax.axis_size...  33.5 us
    ppermute x24, starting transfers between devices, exchange(): lax.ppermute(value, axis, [(i, i ^ distance) for i in range(lax.axis_size...  28.1 us
    all_to_all x6, starting transfers between devices, swap(): return lax.all_to_all(value, 'sz', split_axis=0, concat_axis=0, tiled=True)  28 us
    ppermute x8, starting transfers between devices, edges(): return (lax.ppermute(last, 'sx', up), lax.ppermute(first, 'sx', down))  11.9 us
  transfers between devices with their start and end apart: 38, of which 27 were waited for; matrix products, arithmetic and copies ran while one was open for 1% of the time, Pallas kernels for 13%

profile of v1, /device:TPU:0, one launch (start us, length us, event | category | flops | bytes accessed | tf_op | source)
XLA Modules:
  0.0 464.7 jit_solution(6419367858166181679)
XLA Ops:
  7.6 6.3 %all-to-all-start = ((bf16[8,18,32,256]{3,2,1,0:T(8,128)(2,1)}), bf16[8,18,32,256]{3,2,1,0:T(8,128)(2,1)S(1)}, u32[]{:S(2)}, u32[]{:S(2)}) async-start(bf16[8,18,32,256]{3,2,1,0:T(8,128)(2,1)} %copy-done.26), calls=%async_computation | async-start | bytes 4718592 | tf_op jit(solution)/shard_map/all_to_all | solution.py:494
  17.6 10.3 %shard_map.65 = (s16[8,18,32,256]{3,2,1,0:T(8,128)(2,1)S(1)}, bf16[8,18,32,256]{3,2,1,0:T(8,128)(2,1)S(1)}, s16[8,18,32,256]{3,2,1,0:T(8,128)(2,1)S(1)}, f32[8,128]{1,0:T(8,128)S(1)}) custom-call(f32[18,32,4096]{2,1,0:T(8,128)S(1)} %copy-done.12, bf16[512,256]{1,0:T(8,128)(2,1)S(1)} %get-tuple-element.103.refs_1_, ...), custom_call_target="tpu_custom_call" | custom-call | flops 6039797760 | bytes 16515072 | tf_op jit(solution)/shard_map/pallas_call | solution.py:52
  32.2 36.4 %all-to-all-done.refs_0_.refs_6_.refs_1_ = bf16[8,18,32,256]{3,2,1,0:T(8,128)(2,1)S(1)} async-done(((bf16[8,18,32,256]{3,2,1,0:T(8,128)(2,1)}), bf16[8,18,32,256]{3,2,1,0:T(8,128)(2,1)S(1)}, u32[]{:S(2)}, u32[]{:S(2)}) %all-to-all-start) | async-done | bytes 2359328 | tf_op jit(solution)/shard_map/all_to_all | solution.py:494
  68.6 4.5 all-to-all-start.1
  73.5 4.4 shard_map.66
  80.8 18.3 %collective-permute-done.refs_1_ = bf16[6,256,256]{2,1,0:T(8,128)(2,1)S(1)} collective-permute-done((bf16[6,256,256]{2,1,0:T(8,128)(2,1)S(1)}, bf16[6,256,256]{2,1,0:T(8,128)(2,1)S(1)}, u32[]{:S(2)}, u32[]{:S(2)}) %collective-permute-start) | collective-permute-done | bytes 786464 | tf_op jit(solution)/shard_map/ppermute | solution.py:501
  99.2 16.3 %collective-permute-done.1.refs_3_ = bf16[6,256,256]{2,1,0:T(8,128)(2,1)S(1)} collective-permute-done((bf16[6,256,256]{2,1,0:T(8,128)(2,1)S(1)}, bf16[6,256,256]{2,1,0:T(8,128)(2,1)S(1)}, u32[]{:S(2)}, u32[]{:S(2)}) %collective-permute-start.1) | collective-permute-done | bytes 786464 | tf_op jit(solution)/shard_map/ppermute | solution.py:501
  115.5 4.4 copy-done
  119.8 5.5 %shard_map.67 = (f32[18,256,256]{2,1,0:T(8,128)S(1)}, f32[8,256]{1,0:T(8,128)S(1)}, f32[8,128]{1,0:T(8,128)S(1)}) custom-call(s32[5]{0:T(128)S(1)} %copy-done.29, bf16[6,256,256]{2,1,0:T(8,128)(2,1)S(1)} %collective-permute-done.refs_1_, bf16[18,256,256]{2,1,0:T(8,128)(2,1)S(1)} %get-tuple-element.57.refs_2_.refs_0_, ...), custom_call_target="tpu_custom_call" | custom-call | flops 3019898880 | bytes 23592960 | tf_op jit(solution)/shard_map/pallas_call | solution.py:52
  131.3 4.6 shard_map.68
  161.4 6.7 %shard_map.70 = (f32[18,256,256]{2,1,0:T(8,128)S(1)}, bf16[18,256,256]{2,1,0:T(8,128)(2,1)S(1)}, bf16[6,256,256]{2,1,0:T(8,128)(2,1)S(1)}, bf16[6,256,256]{2,1,0...) custom-call(bf16[8,18,32,256]{3,2,1,0:T(8,128)(2,1)S(1)} %copy-done.4, ...), custom_call_target="tpu_custom_call" | custom-call | flops 1207959552 | bytes 16515072 | tf_op jit(solution)/shard_map/pallas_call | solution.py:52
  174.7 29.9 %all-to-all-done.2.refs_0_.refs_6_.refs_1_ = bf16[8,18,32,256]{3,2,1,0:T(8,128)(2,1)S(1)} async-done(((bf16[8,18,32,256]{3,2,1,0:T(8,128)(2,1)}), bf16[8,18,32,256]{3,2,1,0:T(8,128)(2,1)S(1)}, u32[]{:S(2)}, u32[]{:S(2)}) %all-to-all-start.2) | async-done | bytes 2359328 | tf_op jit(solution)/shard_map/all_to_all | solution.py:494
  204.7 4.5 all-to-all-start.3
  212.2 4.3 shard_map.72
  219.5 11.2 %collective-permute-done.8.refs_1_ = bf16[6,256,256]{2,1,0:T(8,128)(2,1)S(1)} collective-permute-done((bf16[6,256,256]{2,1,0:T(8,128)(2,1)}, bf16[6,256,256]{2,1,0:T(8,128)(2,1)S(1)}, u32[]{:S(2)}, u32[]{:S(2)}) %collective-permute-start.8) | collective-permute-done | bytes 786464 | tf_op jit(solution)/shard_map/ppermute | solution.py:501
  230.7 15.9 %collective-permute-done.9.refs_3_ = bf16[6,256,256]{2,1,0:T(8,128)(2,1)S(1)} collective-permute-done((bf16[6,256,256]{2,1,0:T(8,128)(2,1)}, bf16[6,256,256]{2,1,0:T(8,128)(2,1)S(1)}, u32[]{:S(2)}, u32[]{:S(2)}) %collective-permute-start.9) | collective-permute-done | bytes 786464 | tf_op jit(solution)/shard_map/ppermute | solution.py:501
  246.6 4.4 copy-done.1
  253.3 5.2 %shard_map.73 = (f32[8,256]{1,0:T(8,128)S(1)}, f32[8,128]{1,0:T(8,128)S(1)}) custom-call(s32[5]{0:T(128)S(1)} %copy-done.29, bf16[6,256,256]{2,1,0:T(8,128)(2,1)S(1)} %collective-permute-done.8.refs_1_, bf16[18,256,256]{2,1,0:T(8,128)(2,1)S(1)} %copy-done.18, bf16[6,256,256]{2,1,0:T(8,128)(2,1)S(1)} %collective-permute-done.9.refs_3_, ...), custom_call_target="tpu_custom_call" | custom-call | flops 3019898880 | bytes 18874368 | tf_op jit(solution)/shard_map/pallas_call | solution.py:52
  269.6 10.2 %collective-permute-done.17.refs_3_ = bf16[6,256,256]{2,1,0:T(8,128)(2,1)S(1)} collective-permute-done((bf16[6,256,256]{2,1,0:T(8,128)(2,1)S(1)}, bf16[6,256,256]{2,1,0:T(8,128)(2,1)S(1)}, u32[]{:S(2)}, u32[]{:S(2)}) %collective-permute-start.17) | collective-permute-done | bytes 786464 | tf_op jit(solution)/shard_map/ppermute | solution.py:501
  279.8 5.5 %shard_map.74 = (f32[18,256,256]{2,1,0:T(8,128)S(1)}, f32[8,256]{1,0:T(8,128)S(1)}, f32[8,128]{1,0:T(8,128)S(1)}) custom-call(s32[5]{0:T(128)S(1)} %copy-done.29, bf16[6,256,256]{2,1,0:T(8,128)(2,1)S(1)} %collective-permute-done.16.refs_1_, bf16[18,256,256]{2,1,0:T(8,128)(2,1)S(1)} %get-tuple-element.81.refs_2_.refs_0_, ...), custom_call_target="tpu_custom_call" | custom-call | flops 3019898880 | bytes 23592960 | tf_op jit(solution)/shard_map/pallas_call | solution.py:52
  289.9 4.9 %shard_map.75 = (f32[8,256]{1,0:T(8,128)S(1)}, f32[8,128]{1,0:T(8,128)}) custom-call(f32[18,256,256]{2,1,0:T(8,128)S(1)} %copy-done.6, bf16[8,18,32,256]{3,2,1,0:T(8,128)(2,1)S(1)} %all-to-all-done.2.refs_0_.refs_6_.refs_1_, s16[8,18,32,256]{3,2,1,0:T(8,128)(2,1)} %all-to-all-done.3.refs_2_.refs_1_, f32[8,256]{1,0:T(8,128)S(1)} %get-tuple-element.86.refs_3_, ...), custom_call_target="tpu_custom_call" | custom-call | flops 2359296 | bytes 9437184 | tf_op jit(solution)/shard_map/pallas_call | solution.py:52
  308.1 4.5 all-to-all-start.4
  322.3 6.7 %shard_map.77 = (f32[18,256,256]{2,1,0:T(8,128)S(1)}, bf16[18,256,256]{2,1,0:T(8,128)(2,1)S(1)}, bf16[6,256,256]{2,1,0:T(8,128)(2,1)S(1)}, bf16[6,256,256]{2,1,0...) custom-call(bf16[8,18,32,256]{3,2,1,0:T(8,128)(2,1)S(1)} %all-to-all-done.2.refs_0_.refs_6_.refs_1_, ...), custom_call_target="tpu_custom_call" | custom-call | flops 1207959552 | bytes 16515072 | tf_op jit(solution)/shard_map/pallas_call | solution.py:52
  332.0 18.4 %collective-permute-done.24.refs_1_ = bf16[6,256,256]{2,1,0:T(8,128)(2,1)S(1)} collective-permute-done((bf16[6,256,256]{2,1,0:T(8,128)(2,1)S(1)}, bf16[6,256,256]{2,1,0:T(8,128)(2,1)S(1)}, u32[]{:S(2)}, u32[]{:S(2)}) %collective-permute-start.24) | collective-permute-done | bytes 786464 | tf_op jit(solution)/shard_map/ppermute | solution.py:501
  350.4 13.7 %collective-permute-done.25.refs_3_ = bf16[6,256,256]{2,1,0:T(8,128)(2,1)S(1)} collective-permute-done((bf16[6,256,256]{2,1,0:T(8,128)(2,1)S(1)}, bf16[6,256,256]{2,1,0:T(8,128)(2,1)S(1)}, u32[]{:S(2)}, u32[]{:S(2)}) %collective-permute-start.25) | collective-permute-done | bytes 786464 | tf_op jit(solution)/shard_map/ppermute | solution.py:501
  364.1 4.3 copy-done.2
  368.5 5.2 %shard_map.78 = (f32[8,256]{1,0:T(8,128)S(1)}, f32[8,128]{1,0:T(8,128)S(1)}) custom-call(s32[5]{0:T(128)S(1)} %copy-done.29, bf16[6,256,256]{2,1,0:T(8,128)(2,1)S(1)} %collective-permute-done.24.refs_1_, bf16[18,256,256]{2,1,0:T(8,128)(2,1)S(1)} %get-tuple-element.92.refs_2_.refs_1_, bf16[6,256,256]{2,1,0:T(8,128)(2,1)S(1)} %collective-permute-done.25.refs_3_, ...), custom_call_target="tpu_custom_call" | custom-call | flops 3019898880 | bytes 18874368 | tf_op jit(solution)/shard_map/pallas_call | solution.py:52
  374.9 3.9 collective-permute-start.29
  394.3 4.4 all-to-all-start.5
  399.0 4.4 convert_element_type.43.refs_0_
  403.5 49.9 %all-to-all-done.5 = f16[8,18,32,256]{3,2,1,0:T(8,128)(2,1)} async-done(((f16[8,18,32,256]{3,2,1,0:T(8,128)(2,1)}), f16[8,18,32,256]{3,2,1,0:T(8,128)(2,1)}, u32[]{:S(2)}, u32[]{:S(2)}) %all-to-all-start.5) | async-done | bytes 2359328 | tf_op jit(solution)/shard_map/all_to_all | solution.py:494
  456.5 8.3 %shard_map.80 = (f32[18,32,4096]{2,1,0:T(8,128)}, f32[8,128]{1,0:T(8,128)}) custom-call(f32[8,18,32,256]{3,2,1,0:T(8,128)S(1)} %copy-done.22, f32[8,18,32,256]{3,2,1,0:T(8,128)S(1)} %convert_element_type.45.refs_1_, f32[8,256]{1,0:T(8,128)S(1)} %add.229.refs_3_.refs_2_, f32[8,256]{1,0:T(8,128)S(1)} %add.241.refs_3_.refs_2_, ...), custom_call_target="tpu_custom_call" | custom-call | flops 4831838208 | bytes 18874368 | tf_op jit(solution)/shard_map/pallas_call | solution.py:52
  (165 shorter events, 126.5 us)
Async XLA Ops:
  7.6 61.0 %all-to-all-start = ((bf16[8,18,32,256]{3,2,1,0:T(8,128)(2,1)}), bf16[8,18,32,256]{3,2,1,0:T(8,128)(2,1)S(1)}, u32[]{:S(2)}, u32[]{:S(2)}) async-start(bf16[8,18,32,256]{3,2,1,0:T(8,128)(2,1)} %copy-done.26), calls=%async_computation | async-start | bytes 4718592 | tf_op jit(solution)/shard_map/all_to_all | solution.py:494
  68.6 60.3 %all-to-all-start.1 = ((s16[8,18,32,256]{3,2,1,0:T(8,128)(2,1)}), s16[8,18,32,256]{3,2,1,0:T(8,128)(2,1)}, u32[]{:S(2)}, u32[]{:S(2)}) async-start(s16[8,18,32,256]{3,2,1,0:T(8,128)(2,1)} %copy-done.25), calls=%async_computation.1 | async-start | bytes 4718592 | tf_op jit(solution)/shard_map/all_to_all | solution.py:494
  77.8 21.3 %collective-permute-start = (bf16[6,256,256]{2,1,0:T(8,128)(2,1)S(1)}, bf16[6,256,256]{2,1,0:T(8,128)(2,1)S(1)}, u32[]{:S(2)}, u32[]{:S(2)}) collective-permute-start(bf16[6,256,256]{2,1,0:T(8,128)(2,1)S(1)} %get-tuple-element.59), channel_id=1, source_target_pairs={{0,8},{8,16},{16,24},{24,0},{1,9},{9,17},{17,25},{25,1},{2,10},{10... | collective-permute-start | bytes 2359304 | tf_op jit(solution)/shard_map/ppermute | solution.py:501
  79.4 36.1 %collective-permute-start.1 = (bf16[6,256,256]{2,1,0:T(8,128)(2,1)S(1)}, bf16[6,256,256]{2,1,0:T(8,128)(2,1)S(1)}, u32[]{:S(2)}, u32[]{:S(2)}) collective-permute-start(bf16[6,256,256]{2,1,0:T(8,128)(2,1)S(1)} %get-tuple-element.60), channel_id=1, source_target_pairs={{8,0},{16,8},{24,16},{0,24},{9,1},{17,9},{25,17},{1,25},{10,2},{18... | collective-permute-start | bytes 2359304 | tf_op jit(solution)/shard_map/ppermute | solution.py:501
  137.1 5.4 %collective-permute-start.5 = (f32[8,256]{1,0:T(8,128)S(1)}, f32[8,256]{1,0:T(8,128)S(1)}, u32[]{:S(2)}, u32[]{:S(2)}) collective-permute-start(f32[8,256]{1,0:T(8,128)S(1)} %add.224), channel_id=1, source_target_pairs={{0,6},{1,7},{2,4},{3,5},{4,2},{5,3},{6,0},{7,1},{8,14},{9,15},{10,... | collective-permute-start | bytes 24584 | tf_op jit(solution)/shard_map/ppermute | solution.py:505
  140.6 4.5 collective-permute-start.4
  140.6 4.5 collective-permute-start.3
  146.3 58.4 %all-to-all-start.2 = ((bf16[8,18,32,256]{3,2,1,0:T(8,128)(2,1)}), bf16[8,18,32,256]{3,2,1,0:T(8,128)(2,1)S(1)}, u32[]{:S(2)}, u32[]{:S(2)}) async-start(bf16[8,18,32,256]{3,2,1,0:T(8,128)(2,1)} %get-tuple-element.74), calls=%async_computation.2 | async-start | bytes 4718592 | tf_op jit(solution)/shard_map/all_to_all | solution.py:494
  150.1 3.7 collective-permute-start.6
  153.8 3.7 collective-permute-start.7
  204.7 82.9 %all-to-all-start.3 = ((s16[8,18,32,256]{3,2,1,0:T(8,128)(2,1)}), s16[8,18,32,256]{3,2,1,0:T(8,128)(2,1)}, u32[]{:S(2)}, u32[]{:S(2)}) async-start(s16[8,18,32,256]{3,2,1,0:T(8,128)(2,1)} %get-tuple-element.85), calls=%async_computation.3 | async-start | bytes 4718592 | tf_op jit(solution)/shard_map/all_to_all | solution.py:494
  209.2 21.5 %collective-permute-start.8 = (bf16[6,256,256]{2,1,0:T(8,128)(2,1)}, bf16[6,256,256]{2,1,0:T(8,128)(2,1)S(1)}, u32[]{:S(2)}, u32[]{:S(2)}) collective-permute-start(bf16[6,256,256]{2,1,0:T(8,128)(2,1)} %copy-done.33), channel_id=1, source_target_pairs={{0,8},{8,16},{16,24},{24,0},{1,9},{9,17},{17,25},{25,1},{2,10},{10... | collective-permute-start | bytes 2359304 | tf_op jit(solution)/shard_map/ppermute | solution.py:501
  210.7 35.9 %collective-permute-start.9 = (bf16[6,256,256]{2,1,0:T(8,128)(2,1)}, bf16[6,256,256]{2,1,0:T(8,128)(2,1)S(1)}, u32[]{:S(2)}, u32[]{:S(2)}) collective-permute-start(bf16[6,256,256]{2,1,0:T(8,128)(2,1)} %copy-done.32), channel_id=1, source_target_pairs={{8,0},{16,8},{24,16},{0,24},{9,1},{17,9},{25,17},{1,25},{10,2},{18... | collective-permute-start | bytes 2359304 | tf_op jit(solution)/shard_map/ppermute | solution.py:501
  216.5 53.1 %collective-permute-start.16 = (bf16[6,256,256]{2,1,0:T(8,128)(2,1)S(1)}, bf16[6,256,256]{2,1,0:T(8,128)(2,1)S(1)}, u32[]{:S(2)}, u32[]{:S(2)}) collective-permute-start(bf16[6,256,256]{2,1,0:T(8,128)(2,1)S(1)} %get-tuple-element.80), channel_id=1, source_target_pairs={{0,8},{8,16},{16,24},{24,0},{1,9},{9,17},{17,25},{25,1},{2,10},{10... | collective-permute-start | bytes 2359304 | tf_op jit(solution)/shard_map/ppermute | solution.py:501
  217.2 62.7 %collective-permute-start.17 = (bf16[6,256,256]{2,1,0:T(8,128)(2,1)S(1)}, bf16[6,256,256]{2,1,0:T(8,128)(2,1)S(1)}, u32[]{:S(2)}, u32[]{:S(2)}) collective-permute-start(bf16[6,256,256]{2,1,0:T(8,128)(2,1)S(1)} %get-tuple-element.82), channel_id=1, source_target_pairs={{8,0},{16,8},{24,16},{0,24},{9,1},{17,9},{25,17},{1,25},{10,2},{18... | collective-permute-start | bytes 2359304 | tf_op jit(solution)/shard_map/ppermute | solution.py:501
  259.8 5.4 %collective-permute-start.13 = (f32[8,256]{1,0:T(8,128)S(1)}, f32[8,256]{1,0:T(8,128)S(1)}, u32[]{:S(2)}, u32[]{:S(2)}) collective-permute-start(f32[8,256]{1,0:T(8,128)S(1)} %add.230), channel_id=1, source_target_pairs={{0,6},{1,7},{2,4},{3,5},{4,2},{5,3},{6,0},{7,1},{8,14},{9,15},{10,... | collective-permute-start | bytes 24584 | tf_op jit(solution)/shard_map/ppermute | solution.py:505
  263.5 4.5 collective-permute-start.12
  263.5 4.5 collective-permute-start.11
  268.0 26.8 %collective-permute-start.14 = (f32[8,256]{1,0:T(8,128)S(1)}, f32[8,256]{1,0:T(8,128)S(1)}, u32[]{:S(2)}, u32[]{:S(2)}) collective-permute-start(f32[8,256]{1,0:T(8,128)S(1)} %add_add_fusion.2), channel_id=1, source_target_pairs={{0,8},{8,0},{16,24},{24,16},{1,9},{9,1},{17,25},{25,17},{2,10},{10... | collective-permute-start | bytes 24584 | tf_op jit(solution)/shard_map/ppermute | solution.py:505
  294.9 6.0 %collective-permute-start.15 = (f32[8,256]{1,0:T(8,128)S(1)}, f32[8,256]{1,0:T(8,128)S(1)}, u32[]{:S(2)}, u32[]{:S(2)}) collective-permute-start(f32[8,256]{1,0:T(8,128)S(1)} %add.234), channel_id=1, source_target_pairs={{0,16},{8,24},{16,0},{24,8},{1,17},{9,25},{17,1},{25,9},{2,18},{10... | collective-permute-start | bytes 24584 | tf_op jit(solution)/shard_map/ppermute | solution.py:505
  296.4 5.4 %collective-permute-start.21 = (f32[8,256]{1,0:T(8,128)S(1)}, f32[8,256]{1,0:T(8,128)S(1)}, u32[]{:S(2)}, u32[]{:S(2)}) collective-permute-start(f32[8,256]{1,0:T(8,128)S(1)} %add.236), channel_id=1, source_target_pairs={{0,6},{1,7},{2,4},{3,5},{4,2},{5,3},{6,0},{7,1},{8,14},{9,15},{10,... | collective-permute-start | bytes 24584 | tf_op jit(solution)/shard_map/ppermute | solution.py:505
  299.9 4.5 collective-permute-start.20
  299.9 4.5 collective-permute-start.19
  308.1 86.3 %all-to-all-start.4 = ((f16[8,18,32,256]{3,2,1,0:T(8,128)(2,1)}), f16[8,18,32,256]{3,2,1,0:T(8,128)(2,1)}, u32[]{:S(2)}, u32[]{:S(2)}) async-start(f16[8,18,32,256]{3,2,1,0:T(8,128)(2,1)} %convert_element_type.42), calls=%async_computation.4 | async-start | bytes 4718592 | tf_op jit(solution)/shard_map/all_to_all | solution.py:494
  312.6 3.7 collective-permute-start.22
  329.0 21.4 %collective-permute-start.24 = (bf16[6,256,256]{2,1,0:T(8,128)(2,1)S(1)}, bf16[6,256,256]{2,1,0:T(8,128)(2,1)S(1)}, u32[]{:S(2)}, u32[]{:S(2)}) collective-permute-start(bf16[6,256,256]{2,1,0:T(8,128)(2,1)S(1)} %get-tuple-element.93), channel_id=1, source_target_pairs={{0,8},{8,16},{16,24},{24,0},{1,9},{9,17},{17,25},{25,1},{2,10},{10... | collective-permute-start | bytes 2359304 | tf_op jit(solution)/shard_map/ppermute | solution.py:501
  330.6 33.6 %collective-permute-start.25 = (bf16[6,256,256]{2,1,0:T(8,128)(2,1)S(1)}, bf16[6,256,256]{2,1,0:T(8,128)(2,1)S(1)}, u32[]{:S(2)}, u32[]{:S(2)}) collective-permute-start(bf16[6,256,256]{2,1,0:T(8,128)(2,1)S(1)} %get-tuple-element.94), channel_id=1, source_target_pairs={{8,0},{16,8},{24,16},{0,24},{9,1},{17,9},{25,17},{1,25},{10,2},{18... | collective-permute-start | bytes 2359304 | tf_op jit(solution)/shard_map/ppermute | solution.py:501
  374.9 5.5 %collective-permute-start.29 = (f32[8,256]{1,0:T(8,128)S(1)}, f32[8,256]{1,0:T(8,128)S(1)}, u32[]{:S(2)}, u32[]{:S(2)}) collective-permute-start(f32[8,256]{1,0:T(8,128)S(1)} %add.242), channel_id=1, source_target_pairs={{0,6},{1,7},{2,4},{3,5},{4,2},{5,3},{6,0},{7,1},{8,14},{9,15},{10,... | collective-permute-start | bytes 24584 | tf_op jit(solution)/shard_map/ppermute | solution.py:505
  378.8 4.5 collective-permute-start.28
  378.8 4.5 collective-permute-start.27
  383.4 3.7 collective-permute-start.30
  394.3 59.1 %all-to-all-start.5 = ((f16[8,18,32,256]{3,2,1,0:T(8,128)(2,1)}), f16[8,18,32,256]{3,2,1,0:T(8,128)(2,1)}, u32[]{:S(2)}, u32[]{:S(2)}) async-start(f16[8,18,32,256]{3,2,1,0:T(8,128)(2,1)} %convert_element_type.44), calls=%async_computation.5 | async-start | bytes 4718592 | tf_op jit(solution)/shard_map/all_to_all | solution.py:494
  (43 other events, 358.4 us)

commit v2 on v1

--- a/solution.py
+++ b/solution.py
@@ -25,7 +25,7 @@
         self.token = jnp.zeros((8, 128), F32)
 
 
-def call(order, body, grid, in_specs, out_specs, out_shape, flops, moved, scratch=(), scalars=0):
+def call(order, body, grid, in_specs, out_specs, out_shape, flops, moved, scratch=(), scalars=0, grant=VMEM):
     outs = len(out_shape)
     inputs = len(in_specs)
 
@@ -44,7 +44,7 @@
             scratch_shapes=list(scratch),
         ),
         out_shape=out_shape + [jax.ShapeDtypeStruct((8, 128), F32)],
-        compiler_params=pltpu.CompilerParams(vmem_limit_bytes=VMEM),
+        compiler_params=pltpu.CompilerParams(vmem_limit_bytes=grant),
         cost_estimate=pl.CostEstimate(flops=int(flops), bytes_accessed=int(moved), transcendentals=0),
     )
 
@@ -409,6 +409,7 @@
         2 * count * points * width,
         8 * count * points * width,
         scratch=[pltpu.VMEM((8, width), F32)],
+        grant=58 * 2**20,
     )(image, high, low, sums, norm)
 
 
@@ -573,7 +574,9 @@
         sums = apply_last(
             self.order, self.offsets, self.before, self.two, self.after, self.coupling, self.wave, self.residual, self.norm
         )
-        self.second = total_mode(total_span(sums))
+        spans = total_span(sums)
+        self.order.token = spans
+        self.second = total_mode(spans)
 
     def combine(self):
         sent = combine(self.order, self.amount, self.one, self.two, self.first, self.second, self.peers)
@@ -581,8 +584,22 @@
 
 
 PLAN = (
-    "send_high0 send_low0 begin0 apply0 rest0 gate_high1 again0 gate_low1 begin1 finish0 "
-    "apply1 rest1 combine0 again1 finish1 combine1"
+    ("send_high", 0),
+    ("send_low", 0),
+    ("begin", 0),
+    ("apply", 0),
+    ("rest", 0),
+    ("gate_high", 1),
+    ("again", 0),
+    ("finish", 0),
+    ("gate_low", 1),
+    ("begin", 1),
+    ("apply", 1),
+    ("rest", 1),
+    ("combine", 0),
+    ("again", 1),
+    ("finish", 1),
+    ("combine", 1),
 )
 
 
@@ -596,8 +613,8 @@
     made = pack(order, right_side, [chunk.pick for chunk, _ in others], tuple(part for _, part in others), peers)
     for (chunk, part), value in zip(others, made):
         setattr(chunk, "low" if part else "high", value)
-    for step in PLAN.split():
-        getattr(chunks[int(step[-1])], step[:-1])()
+    for step, which in PLAN:
+        getattr(chunks[which], step)()
     place = jnp.concatenate([c.pick.T for c in chunks], axis=0)
     return spread(order, [c.value for c in chunks], [c.first for c in chunks], [c.second for c in chunks], place)
 

time: 466 us -> 465 us (level)
  local copies, waits for them, and re-layouts: 51.9 us -> 47.1 us
    all_to_all x6, waiting for transfers between devices: 116 us -> 86.3 us  [swap(): return lax.all_to_all(value, 'sz', split_axis=0, concat_axis=0, tiled=True)]
    ppermute x8, waiting for transfers between devices: 104 us -> 132 us  [edges(): return (lax.ppermute(last, 'sx', up), lax.ppermute(first, 'sx', down))]
    unnamed x74 -> x78, local copies, waits for them, and re-layouts: 51.8 us -> 47 us
  transfers between devices with their start and end apart: 38 -> 38, of which waited for: 27 -> 28; matrix products, arithmetic and copies ran while one was open for 1% -> 2% of each run, Pallas kernels for 13% -> 14%
where the time goes in v2:
time: 465 us; the launch traced here: 464 us
  waiting for transfers between devices  253 us (54%)
  Pallas kernels  82.9 us (18%)
  starting transfers between devices  66.1 us (14%)
  local copies, waits for them, and re-layouts  47.1 us (10%)
  other arithmetic  13.9 us (3%)
    ppermute x8, waiting for transfers between devices, edges(): return (lax.ppermute(last, 'sx', up), lax.ppermute(first, 'sx', down))  132 us
    all_to_all x6, waiting for transfers between devices, swap(): return lax.all_to_all(value, 'sz', split_axis=0, concat_axis=0, tiled=True)  86.3 us
    pallas_call x15, Pallas kernels, run(): *given, order.token = kernel(*args, order.token)  81.7 us
    unnamed x78, local copies, waits for them, and re-layouts  47 us
    ppermute x24, waiting for transfers between devices, exchange(): lax.ppermute(value, axis, [(i, i ^ distance) for i in range(lax.axis_size...  34.7 us
    all_to_all x6, starting transfers between devices, swap(): return lax.all_to_all(value, 'sz', split_axis=0, concat_axis=0, tiled=True)  28.1 us
    ppermute x24, starting transfers between devices, exchange(): lax.ppermute(value, axis, [(i, i ^ distance) for i in range(lax.axis_size...  26.1 us
    ppermute x8, starting transfers between devices, edges(): return (lax.ppermute(last, 'sx', up), lax.ppermute(first, 'sx', down))  11.9 us
  transfers between devices with their start and end apart: 38, of which 28 were waited for; matrix products, arithmetic and copies ran while one was open for 2% of the time, Pallas kernels for 14%

profile of v2, /device:TPU:0, one launch (start us, length us, event | category | flops | bytes accessed | tf_op | source)
XLA Modules:
  0.0 463.8 jit_solution(11592365106199880846)
XLA Ops:
  7.6 6.3 %all-to-all-start = ((bf16[8,18,32,256]{3,2,1,0:T(8,128)(2,1)}), bf16[8,18,32,256]{3,2,1,0:T(8,128)(2,1)S(1)}, u32[]{:S(2)}, u32[]{:S(2)}) async-start(bf16[8,18,32,256]{3,2,1,0:T(8,128)(2,1)} %copy-done.24), calls=%async_computation | async-start | bytes 4718592 | tf_op jit(solution)/shard_map/all_to_all | solution.py:495
  17.6 10.3 %shard_map.65 = (s16[8,18,32,256]{3,2,1,0:T(8,128)(2,1)S(1)}, bf16[8,18,32,256]{3,2,1,0:T(8,128)(2,1)S(1)}, s16[8,18,32,256]{3,2,1,0:T(8,128)(2,1)S(1)}, f32[8,128]{1,0:T(8,128)S(1)}) custom-call(f32[18,32,4096]{2,1,0:T(8,128)S(1)} %copy-done.13, bf16[512,256]{1,0:T(8,128)(2,1)S(1)} %get-tuple-element.99.refs_1_, ...), custom_call_target="tpu_custom_call" | custom-call | flops 6039797760 | bytes 16515072 | tf_op jit(solution)/shard_map/pallas_call | solution.py:52
  32.3 36.3 %all-to-all-done.refs_0_.refs_6_.refs_1_ = bf16[8,18,32,256]{3,2,1,0:T(8,128)(2,1)S(1)} async-done(((bf16[8,18,32,256]{3,2,1,0:T(8,128)(2,1)}), bf16[8,18,32,256]{3,2,1,0:T(8,128)(2,1)S(1)}, u32[]{:S(2)}, u32[]{:S(2)}) %all-to-all-start) | async-done | bytes 2359328 | tf_op jit(solution)/shard_map/all_to_all | solution.py:495
  68.6 4.5 all-to-all-start.1
  73.4 4.4 shard_map.66
  80.8 18.3 %collective-permute-done.refs_1_ = bf16[6,256,256]{2,1,0:T(8,128)(2,1)S(1)} collective-permute-done((bf16[6,256,256]{2,1,0:T(8,128)(2,1)S(1)}, bf16[6,256,256]{2,1,0:T(8,128)(2,1)S(1)}, u32[]{:S(2)}, u32[]{:S(2)}) %collective-permute-start) | collective-permute-done | bytes 786464 | tf_op jit(solution)/shard_map/ppermute | solution.py:502
  99.1 16.3 %collective-permute-done.1.refs_3_ = bf16[6,256,256]{2,1,0:T(8,128)(2,1)S(1)} collective-permute-done((bf16[6,256,256]{2,1,0:T(8,128)(2,1)S(1)}, bf16[6,256,256]{2,1,0:T(8,128)(2,1)S(1)}, u32[]{:S(2)}, u32[]{:S(2)}) %collective-permute-start.1) | collective-permute-done | bytes 786464 | tf_op jit(solution)/shard_map/ppermute | solution.py:502
  115.5 4.4 copy-done
  119.8 5.5 %shard_map.67 = (f32[18,256,256]{2,1,0:T(8,128)S(1)}, f32[8,256]{1,0:T(8,128)S(1)}, f32[8,128]{1,0:T(8,128)S(1)}) custom-call(s32[5]{0:T(128)S(1)} %copy-done.27, bf16[6,256,256]{2,1,0:T(8,128)(2,1)S(1)} %collective-permute-done.refs_1_, bf16[18,256,256]{2,1,0:T(8,128)(2,1)S(1)} %get-tuple-element.55.refs_2_.refs_0_, ...), custom_call_target="tpu_custom_call" | custom-call | flops 3019898880 | bytes 23592960 | tf_op jit(solution)/shard_map/pallas_call | solution.py:52
  130.1 6.0 %shard_map.68 = (f32[8,256]{1,0:T(8,128)}, f32[8,128]{1,0:T(8,128)}) custom-call(f32[18,256,256]{2,1,0:T(8,128)} %copy-done.10, bf16[8,18,32,256]{3,2,1,0:T(8,128)(2,1)} %copy-done.6, s16[8,18,32,256]{3,2,1,0:T(8,128)(2,1)} %all-to-all-done.1.refs_2_.refs_1_, f32[8,256]{1,0:T(8,128)} %copy-done.30, f32[8,256]{1,0:T(8,128)} %copy-done.29, f32[8,128]{1,0:T(8,128)} %copy-done.33), custom_call_target="tpu_custom_call" | custom-call | flops 2359296 | bytes 9437184 | tf_op jit(solution)/shard_map/pallas_call | solution.py:52
  162.6 6.7 %shard_map.70 = (f32[18,256,256]{2,1,0:T(8,128)S(1)}, bf16[18,256,256]{2,1,0:T(8,128)(2,1)S(1)}, bf16[6,256,256]{2,1,0:T(8,128)(2,1)S(1)}, bf16[6,256,256]{2,1,0...) custom-call(bf16[8,18,32,256]{3,2,1,0:T(8,128)(2,1)S(1)} %copy-done.7, ...), custom_call_target="tpu_custom_call" | custom-call | flops 1207959552 | bytes 16515072 | tf_op jit(solution)/shard_map/pallas_call | solution.py:52
  172.3 18.5 %collective-permute-done.8.refs_1_ = bf16[6,256,256]{2,1,0:T(8,128)(2,1)S(1)} collective-permute-done((bf16[6,256,256]{2,1,0:T(8,128)(2,1)S(1)}, bf16[6,256,256]{2,1,0:T(8,128)(2,1)S(1)}, u32[]{:S(2)}, u32[]{:S(2)}) %collective-permute-start.8) | collective-permute-done | bytes 786464 | tf_op jit(solution)/shard_map/ppermute | solution.py:502
  190.8 13.2 %collective-permute-done.9.refs_3_ = bf16[6,256,256]{2,1,0:T(8,128)(2,1)S(1)} collective-permute-done((bf16[6,256,256]{2,1,0:T(8,128)(2,1)S(1)}, bf16[6,256,256]{2,1,0:T(8,128)(2,1)S(1)}, u32[]{:S(2)}, u32[]{:S(2)}) %collective-permute-start.9) | collective-permute-done | bytes 786464 | tf_op jit(solution)/shard_map/ppermute | solution.py:502
  203.9 4.3 copy-done.1
  208.3 5.8 %shard_map.71 = (f32[8,256]{1,0:T(8,128)S(1)}, f32[8,128]{1,0:T(8,128)}) custom-call(s32[5]{0:T(128)S(1)} %copy-done.27, bf16[6,256,256]{2,1,0:T(8,128)(2,1)S(1)} %collective-permute-done.8.refs_1_, bf16[18,256,256]{2,1,0:T(8,128)(2,1)S(1)} %get-tuple-element.67.refs_2_.refs_1_, bf16[6,256,256]{2,1,0:T(8,128)(2,1)S(1)} %collective-permute-done.9.refs_3_, ...), custom_call_target="tpu_custom_call" | custom-call | flops 3019898880 | bytes 18874368 | tf_op jit(solution)/shard_map/pallas_call | solution.py:52
  224.9 4.5 all-to-all-start.3
  229.5 4.4 shard_map.73
  237.4 17.7 %collective-permute-done.16.refs_1_ = bf16[6,256,256]{2,1,0:T(8,128)(2,1)S(1)} collective-permute-done((bf16[6,256,256]{2,1,0:T(8,128)(2,1)S(1)}, bf16[6,256,256]{2,1,0:T(8,128)(2,1)S(1)}, u32[]{:S(2)}, u32[]{:S(2)}) %collective-permute-start.16) | collective-permute-done | bytes 786464 | tf_op jit(solution)/shard_map/ppermute | solution.py:502
  255.1 16.5 %collective-permute-done.17.refs_3_ = bf16[6,256,256]{2,1,0:T(8,128)(2,1)S(1)} collective-permute-done((bf16[6,256,256]{2,1,0:T(8,128)(2,1)S(1)}, bf16[6,256,256]{2,1,0:T(8,128)(2,1)S(1)}, u32[]{:S(2)}, u32[]{:S(2)}) %collective-permute-start.17) | collective-permute-done | bytes 786464 | tf_op jit(solution)/shard_map/ppermute | solution.py:502
  271.6 4.4 copy-done.2
  276.0 5.5 %shard_map.74 = (f32[18,256,256]{2,1,0:T(8,128)S(1)}, f32[8,256]{1,0:T(8,128)S(1)}, f32[8,128]{1,0:T(8,128)S(1)}) custom-call(s32[5]{0:T(128)S(1)} %copy-done.27, bf16[6,256,256]{2,1,0:T(8,128)(2,1)S(1)} %collective-permute-done.16.refs_1_, bf16[18,256,256]{2,1,0:T(8,128)(2,1)S(1)} %get-tuple-element.78.refs_2_.refs_0_, ...), custom_call_target="tpu_custom_call" | custom-call | flops 3019898880 | bytes 23592960 | tf_op jit(solution)/shard_map/pallas_call | solution.py:52
  286.3 6.8 %shard_map.75 = (f32[8,256]{1,0:T(8,128)}, f32[8,128]{1,0:T(8,128)}) custom-call(f32[18,256,256]{2,1,0:T(8,128)} %copy-done.8, bf16[8,18,32,256]{3,2,1,0:T(8,128)(2,1)} %copy-done.4, s16[8,18,32,256]{3,2,1,0:T(8,128)(2,1)} %all-to-all-done.3.refs_2_.refs_1_, f32[8,256]{1,0:T(8,128)} %copy-done.31, f32[8,256]{1,0:T(8,128)} %copy-done.28, f32[8,128]{1,0:T(8,128)} %copy-done.34), custom_call_target="tpu_custom_call" | custom-call | flops 2359296 | bytes 9437184 | tf_op jit(solution)/shard_map/pallas_call | solution.py:52
  306.8 4.7 %all-to-all-start.4 = ((f16[8,18,32,256]{3,2,1,0:T(8,128)(2,1)}), f16[8,18,32,256]{3,2,1,0:T(8,128)(2,1)}, u32[]{:S(2)}, u32[]{:S(2)}) async-start(f16[8,18,32,256]{3,2,1,0:T(8,128)(2,1)} %convert_element_type.42), calls=%async_computation.4 | async-start | bytes 4718592 | tf_op jit(solution)/shard_map/all_to_all | solution.py:495
  321.1 6.7 %shard_map.77 = (f32[18,256,256]{2,1,0:T(8,128)S(1)}, bf16[18,256,256]{2,1,0:T(8,128)(2,1)S(1)}, bf16[6,256,256]{2,1,0:T(8,128)(2,1)S(1)}, bf16[6,256,256]{2,1,0...) custom-call(bf16[8,18,32,256]{3,2,1,0:T(8,128)(2,1)S(1)} %copy-done.5, ...), custom_call_target="tpu_custom_call" | custom-call | flops 1207959552 | bytes 16515072 | tf_op jit(solution)/shard_map/pallas_call | solution.py:52
  330.8 18.5 %collective-permute-done.24.refs_1_ = bf16[6,256,256]{2,1,0:T(8,128)(2,1)S(1)} collective-permute-done((bf16[6,256,256]{2,1,0:T(8,128)(2,1)S(1)}, bf16[6,256,256]{2,1,0:T(8,128)(2,1)S(1)}, u32[]{:S(2)}, u32[]{:S(2)}) %collective-permute-start.24) | collective-permute-done | bytes 786464 | tf_op jit(solution)/shard_map/ppermute | solution.py:502
  349.3 13.3 %collective-permute-done.25.refs_3_ = bf16[6,256,256]{2,1,0:T(8,128)(2,1)S(1)} collective-permute-done((bf16[6,256,256]{2,1,0:T(8,128)(2,1)S(1)}, bf16[6,256,256]{2,1,0:T(8,128)(2,1)S(1)}, u32[]{:S(2)}, u32[]{:S(2)}) %collective-permute-start.25) | collective-permute-done | bytes 786464 | tf_op jit(solution)/shard_map/ppermute | solution.py:502
  362.6 4.3 copy-done.3
  367.0 5.8 %shard_map.78 = (f32[8,256]{1,0:T(8,128)S(1)}, f32[8,128]{1,0:T(8,128)}) custom-call(s32[5]{0:T(128)S(1)} %copy-done.27, bf16[6,256,256]{2,1,0:T(8,128)(2,1)S(1)} %collective-permute-done.24.refs_1_, bf16[18,256,256]{2,1,0:T(8,128)(2,1)S(1)} %get-tuple-element.89.refs_2_.refs_1_, bf16[6,256,256]{2,1,0:T(8,128)(2,1)S(1)} %collective-permute-done.25.refs_3_, ...), custom_call_target="tpu_custom_call" | custom-call | flops 3019898880 | bytes 18874368 | tf_op jit(solution)/shard_map/pallas_call | solution.py:52
  393.4 4.4 all-to-all-start.5
  398.1 4.4 convert_element_type.43.refs_0_
  402.5 49.9 %all-to-all-done.5 = f16[8,18,32,256]{3,2,1,0:T(8,128)(2,1)} async-done(((f16[8,18,32,256]{3,2,1,0:T(8,128)(2,1)}), f16[8,18,32,256]{3,2,1,0:T(8,128)(2,1)}, u32[]{:S(2)}, u32[]{:S(2)}) %all-to-all-start.5) | async-done | bytes 2359328 | tf_op jit(solution)/shard_map/all_to_all | solution.py:495
  455.5 8.3 %shard_map.80 = (f32[18,32,4096]{2,1,0:T(8,128)}, f32[8,128]{1,0:T(8,128)}) custom-call(f32[8,18,32,256]{3,2,1,0:T(8,128)S(1)} %copy-done.22, f32[8,18,32,256]{3,2,1,0:T(8,128)S(1)} %convert_element_type.45.refs_1_, f32[8,256]{1,0:T(8,128)S(1)} %add.229.refs_3_.refs_2_, f32[8,256]{1,0:T(8,128)S(1)} %add.241.refs_3_.refs_2_, ...), custom_call_target="tpu_custom_call" | custom-call | flops 4831838208 | bytes 18874368 | tf_op jit(solution)/shard_map/pallas_call | solution.py:52
  (169 shorter events, 122.4 us)
Async XLA Ops:
  7.6 61.0 %all-to-all-start = ((bf16[8,18,32,256]{3,2,1,0:T(8,128)(2,1)}), bf16[8,18,32,256]{3,2,1,0:T(8,128)(2,1)S(1)}, u32[]{:S(2)}, u32[]{:S(2)}) async-start(bf16[8,18,32,256]{3,2,1,0:T(8,128)(2,1)} %copy-done.24), calls=%async_computation | async-start | bytes 4718592 | tf_op jit(solution)/shard_map/all_to_all | solution.py:495
  68.6 61.5 %all-to-all-start.1 = ((s16[8,18,32,256]{3,2,1,0:T(8,128)(2,1)}), s16[8,18,32,256]{3,2,1,0:T(8,128)(2,1)}, u32[]{:S(2)}, u32[]{:S(2)}) async-start(s16[8,18,32,256]{3,2,1,0:T(8,128)(2,1)} %copy-done.23), calls=%async_computation.1 | async-start | bytes 4718592 | tf_op jit(solution)/shard_map/all_to_all | solution.py:495
  77.8 21.3 %collective-permute-start = (bf16[6,256,256]{2,1,0:T(8,128)(2,1)S(1)}, bf16[6,256,256]{2,1,0:T(8,128)(2,1)S(1)}, u32[]{:S(2)}, u32[]{:S(2)}) collective-permute-start(bf16[6,256,256]{2,1,0:T(8,128)(2,1)S(1)} %get-tuple-element.57), channel_id=1, source_target_pairs={{0,8},{8,16},{16,24},{24,0},{1,9},{9,17},{17,25},{25,1},{2,10},{10... | collective-permute-start | bytes 2359304 | tf_op jit(solution)/shard_map/ppermute | solution.py:502
  79.4 36.1 %collective-permute-start.1 = (bf16[6,256,256]{2,1,0:T(8,128)(2,1)S(1)}, bf16[6,256,256]{2,1,0:T(8,128)(2,1)S(1)}, u32[]{:S(2)}, u32[]{:S(2)}) collective-permute-start(bf16[6,256,256]{2,1,0:T(8,128)(2,1)S(1)} %get-tuple-element.58), channel_id=1, source_target_pairs={{8,0},{16,8},{24,16},{0,24},{9,1},{17,9},{25,17},{1,25},{10,2},{18... | collective-permute-start | bytes 2359304 | tf_op jit(solution)/shard_map/ppermute | solution.py:502
  138.2 5.4 %collective-permute-start.5 = (f32[8,256]{1,0:T(8,128)S(1)}, f32[8,256]{1,0:T(8,128)S(1)}, u32[]{:S(2)}, u32[]{:S(2)}) collective-permute-start(f32[8,256]{1,0:T(8,128)S(1)} %add.224), channel_id=1, source_target_pairs={{0,6},{1,7},{2,4},{3,5},{4,2},{5,3},{6,0},{7,1},{8,14},{9,15},{10,... | collective-permute-start | bytes 24584 | tf_op jit(solution)/shard_map/ppermute | solution.py:506
  141.7 4.5 collective-permute-start.4
  141.7 4.5 collective-permute-start.3
  147.5 77.4 %all-to-all-start.2 = ((bf16[8,18,32,256]{3,2,1,0:T(8,128)(2,1)}), bf16[8,18,32,256]{3,2,1,0:T(8,128)(2,1)S(1)}, u32[]{:S(2)}, u32[]{:S(2)}) async-start(bf16[8,18,32,256]{3,2,1,0:T(8,128)(2,1)} %get-tuple-element.74), calls=%async_computation.2 | async-start | bytes 4718592 | tf_op jit(solution)/shard_map/all_to_all | solution.py:495
  151.3 3.7 collective-permute-start.6
  155.0 3.7 collective-permute-start.7
  169.3 21.4 %collective-permute-start.8 = (bf16[6,256,256]{2,1,0:T(8,128)(2,1)S(1)}, bf16[6,256,256]{2,1,0:T(8,128)(2,1)S(1)}, u32[]{:S(2)}, u32[]{:S(2)}) collective-permute-start(bf16[6,256,256]{2,1,0:T(8,128)(2,1)S(1)} %get-tuple-element.68), channel_id=1, source_target_pairs={{0,8},{8,16},{16,24},{24,0},{1,9},{9,17},{17,25},{25,1},{2,10},{10... | collective-permute-start | bytes 2359304 | tf_op jit(solution)/shard_map/ppermute | solution.py:502
  170.9 33.1 %collective-permute-start.9 = (bf16[6,256,256]{2,1,0:T(8,128)(2,1)S(1)}, bf16[6,256,256]{2,1,0:T(8,128)(2,1)S(1)}, u32[]{:S(2)}, u32[]{:S(2)}) collective-permute-start(bf16[6,256,256]{2,1,0:T(8,128)(2,1)S(1)} %get-tuple-element.69), channel_id=1, source_target_pairs={{8,0},{16,8},{24,16},{0,24},{9,1},{17,9},{25,17},{1,25},{10,2},{18... | collective-permute-start | bytes 2359304 | tf_op jit(solution)/shard_map/ppermute | solution.py:502
  215.4 5.4 %collective-permute-start.13 = (f32[8,256]{1,0:T(8,128)S(1)}, f32[8,256]{1,0:T(8,128)S(1)}, u32[]{:S(2)}, u32[]{:S(2)}) collective-permute-start(f32[8,256]{1,0:T(8,128)S(1)} %add.230), channel_id=1, source_target_pairs={{0,6},{1,7},{2,4},{3,5},{4,2},{5,3},{6,0},{7,1},{8,14},{9,15},{10,... | collective-permute-start | bytes 24584 | tf_op jit(solution)/shard_map/ppermute | solution.py:506
  219.2 4.5 collective-permute-start.12
  219.2 4.5 collective-permute-start.11
  224.9 61.4 %all-to-all-start.3 = ((s16[8,18,32,256]{3,2,1,0:T(8,128)(2,1)}), s16[8,18,32,256]{3,2,1,0:T(8,128)(2,1)}, u32[]{:S(2)}, u32[]{:S(2)}) async-start(s16[8,18,32,256]{3,2,1,0:T(8,128)(2,1)} %get-tuple-element.82), calls=%async_computation.3 | async-start | bytes 4718592 | tf_op jit(solution)/shard_map/all_to_all | solution.py:495
  233.8 21.3 %collective-permute-start.16 = (bf16[6,256,256]{2,1,0:T(8,128)(2,1)S(1)}, bf16[6,256,256]{2,1,0:T(8,128)(2,1)S(1)}, u32[]{:S(2)}, u32[]{:S(2)}) collective-permute-start(bf16[6,256,256]{2,1,0:T(8,128)(2,1)S(1)} %get-tuple-element.77), channel_id=1, source_target_pairs={{0,8},{8,16},{16,24},{24,0},{1,9},{9,17},{17,25},{25,1},{2,10},{10... | collective-permute-start | bytes 2359304 | tf_op jit(solution)/shard_map/ppermute | solution.py:502
  235.4 36.2 %collective-permute-start.17 = (bf16[6,256,256]{2,1,0:T(8,128)(2,1)S(1)}, bf16[6,256,256]{2,1,0:T(8,128)(2,1)S(1)}, u32[]{:S(2)}, u32[]{:S(2)}) collective-permute-start(bf16[6,256,256]{2,1,0:T(8,128)(2,1)S(1)} %get-tuple-element.79), channel_id=1, source_target_pairs={{8,0},{16,8},{24,16},{0,24},{9,1},{17,9},{25,17},{1,25},{10,2},{18... | collective-permute-start | bytes 2359304 | tf_op jit(solution)/shard_map/ppermute | solution.py:502
  236.8 56.2 %collective-permute-start.14 = (f32[8,256]{1,0:T(8,128)S(1)}, f32[8,256]{1,0:T(8,128)S(1)}, u32[]{:S(2)}, u32[]{:S(2)}) collective-permute-start(f32[8,256]{1,0:T(8,128)S(1)} %copy-done.36), channel_id=1, source_target_pairs={{0,8},{8,0},{16,24},{24,16},{1,9},{9,1},{17,25},{25,17},{2,10},{10... | collective-permute-start | bytes 24584 | tf_op jit(solution)/shard_map/ppermute | solution.py:506
  293.1 6.5 %collective-permute-start.15 = (f32[8,256]{1,0:T(8,128)S(1)}, f32[8,256]{1,0:T(8,128)S(1)}, u32[]{:S(2)}, u32[]{:S(2)}) collective-permute-start(f32[8,256]{1,0:T(8,128)S(1)} %add.234), channel_id=1, source_target_pairs={{0,16},{8,24},{16,0},{24,8},{1,17},{9,25},{17,1},{25,9},{2,18},{10... | collective-permute-start | bytes 24584 | tf_op jit(solution)/shard_map/ppermute | solution.py:506
  295.1 5.4 %collective-permute-start.21 = (f32[8,256]{1,0:T(8,128)S(1)}, f32[8,256]{1,0:T(8,128)S(1)}, u32[]{:S(2)}, u32[]{:S(2)}) collective-permute-start(f32[8,256]{1,0:T(8,128)S(1)} %add.236), channel_id=1, source_target_pairs={{0,6},{1,7},{2,4},{3,5},{4,2},{5,3},{6,0},{7,1},{8,14},{9,15},{10,... | collective-permute-start | bytes 24584 | tf_op jit(solution)/shard_map/ppermute | solution.py:506
  298.6 4.5 collective-permute-start.20
  298.6 4.5 collective-permute-start.19
  306.8 86.7 %all-to-all-start.4 = ((f16[8,18,32,256]{3,2,1,0:T(8,128)(2,1)}), f16[8,18,32,256]{3,2,1,0:T(8,128)(2,1)}, u32[]{:S(2)}, u32[]{:S(2)}) async-start(f16[8,18,32,256]{3,2,1,0:T(8,128)(2,1)} %convert_element_type.42), calls=%async_computation.4 | async-start | bytes 4718592 | tf_op jit(solution)/shard_map/all_to_all | solution.py:495
  311.4 3.7 collective-permute-start.22
  327.8 21.4 %collective-permute-start.24 = (bf16[6,256,256]{2,1,0:T(8,128)(2,1)S(1)}, bf16[6,256,256]{2,1,0:T(8,128)(2,1)S(1)}, u32[]{:S(2)}, u32[]{:S(2)}) collective-permute-start(bf16[6,256,256]{2,1,0:T(8,128)(2,1)S(1)} %get-tuple-element.90), channel_id=1, source_target_pairs={{0,8},{8,16},{16,24},{24,0},{1,9},{9,17},{17,25},{25,1},{2,10},{10... | collective-permute-start | bytes 2359304 | tf_op jit(solution)/shard_map/ppermute | solution.py:502
  329.4 33.2 %collective-permute-start.25 = (bf16[6,256,256]{2,1,0:T(8,128)(2,1)S(1)}, bf16[6,256,256]{2,1,0:T(8,128)(2,1)S(1)}, u32[]{:S(2)}, u32[]{:S(2)}) collective-permute-start(bf16[6,256,256]{2,1,0:T(8,128)(2,1)S(1)} %get-tuple-element.91), channel_id=1, source_target_pairs={{8,0},{16,8},{24,16},{0,24},{9,1},{17,9},{25,17},{1,25},{10,2},{18... | collective-permute-start | bytes 2359304 | tf_op jit(solution)/shard_map/ppermute | solution.py:502
  374.0 5.5 %collective-permute-start.29 = (f32[8,256]{1,0:T(8,128)S(1)}, f32[8,256]{1,0:T(8,128)S(1)}, u32[]{:S(2)}, u32[]{:S(2)}) collective-permute-start(f32[8,256]{1,0:T(8,128)S(1)} %add.242), channel_id=1, source_target_pairs={{0,6},{1,7},{2,4},{3,5},{4,2},{5,3},{6,0},{7,1},{8,14},{9,15},{10,... | collective-permute-start | bytes 24584 | tf_op jit(solution)/shard_map/ppermute | solution.py:506
  377.9 4.5 collective-permute-start.28
  377.9 4.5 collective-permute-start.27
  382.5 3.7 collective-permute-start.30
  393.4 59.1 %all-to-all-start.5 = ((f16[8,18,32,256]{3,2,1,0:T(8,128)(2,1)}), f16[8,18,32,256]{3,2,1,0:T(8,128)(2,1)}, u32[]{:S(2)}, u32[]{:S(2)}) async-start(f16[8,18,32,256]{3,2,1,0:T(8,128)(2,1)} %convert_element_type.44), calls=%async_computation.5 | async-start | bytes 4718592 | tf_op jit(solution)/shard_map/all_to_all | solution.py:495
  (45 other events, 447.6 us)

commit v3 on v2

--- a/solution.py
+++ b/solution.py
@@ -25,7 +25,7 @@
         self.token = jnp.zeros((8, 128), F32)
 
 
-def call(order, body, grid, in_specs, out_specs, out_shape, flops, moved, scratch=(), scalars=0, grant=VMEM):
+def call(order, body, grid, in_specs, out_specs, out_shape, flops, moved, scratch=(), scalars=0):
     outs = len(out_shape)
     inputs = len(in_specs)
 
@@ -44,7 +44,7 @@
             scratch_shapes=list(scratch),
         ),
         out_shape=out_shape + [jax.ShapeDtypeStruct((8, 128), F32)],
-        compiler_params=pltpu.CompilerParams(vmem_limit_bytes=grant),
+        compiler_params=pltpu.CompilerParams(vmem_limit_bytes=VMEM),
         cost_estimate=pl.CostEstimate(flops=int(flops), bytes_accessed=int(moved), transcendentals=0),
     )
 
@@ -409,7 +409,6 @@
         2 * count * points * width,
         8 * count * points * width,
         scratch=[pltpu.VMEM((8, width), F32)],
-        grant=58 * 2**20,
     )(image, high, low, sums, norm)
 
 
@@ -450,7 +449,7 @@
     values, firsts, seconds = refs[:n], refs[n : 2 * n], refs[2 * n : 3 * n]
     place_ref, out_ref, scale_ref = refs[3 * n :]
     peers, modes, rows, _ = values[0].shape
-    width = place_ref.shape[1]
+    width = out_ref.shape[2] // peers
 
     @pl.when(pl.program_id(0) == 0)
     def _():
@@ -461,21 +460,28 @@
             scale = jnp.where((side >= first) & (side < first + amount), top, scale)
         scale_ref[0:1] = scale
 
-    joined = jnp.concatenate([v[...].reshape(peers * modes * rows, v.shape[3]) for v in values], axis=1)
-    high = joined.astype(BF16)
-    low = (joined - high.astype(F32)).astype(BF16)
-    moved = (dot(high, place_ref[...]) + dot(low, place_ref[...])) * scale_ref[0:1]
-    for peer in range(peers):
-        for mode in range(modes):
-            at = (peer * modes + mode) * rows
-            out_ref[mode, :, peer * width : (peer + 1) * width] = moved[at : at + rows]
-
-
-def spread(order, values, firsts, seconds, place):
+    groups = min(v.shape[3] for v in values) // 128 or 1
+    flat = [v[...].reshape(peers * modes * rows, v.shape[3]) for v in values]
+    for group in range(groups):
+        cuts = [v.shape[1] // groups for v in flat]
+        joined = jnp.concatenate([v[:, group * cut : (group + 1) * cut] for v, cut in zip(flat, cuts)], axis=1)
+        high = joined.astype(BF16)
+        low = (joined - high.astype(F32)).astype(BF16)
+        span = width // groups
+        moved = dot(high, place_ref[...]) + dot(low, place_ref[...])
+        moved = moved * scale_ref[0:1, group * span : (group + 1) * span]
+        for peer in range(peers):
+            for mode in range(modes):
+                at = (peer * modes + mode) * rows
+                left = peer * width + group * span
+                out_ref[mode, :, left : left + span] = moved[at : at + rows]
+
+
+def spread(order, values, firsts, seconds, place, spans):
     peers, count, rows, _ = values[0].shape
     step = STEP
+    columns = peers * spans * R
     width = place.shape[1]
-    columns = peers * width
     return call(
         order,
         spread_body,
@@ -487,7 +493,7 @@
         [jax.ShapeDtypeStruct((count, rows, columns), F32)],
         4 * count * rows * columns * width,
         8 * count * rows * columns,
-        scratch=[pltpu.VMEM((8, width), F32)],
+        scratch=[pltpu.VMEM((8, spans * R), F32)],
     )(*values, *firsts, *seconds, place)
 
 
@@ -570,13 +576,14 @@
         )
         self.before, self.after = edges(first, last)
 
+    def settle(self):
+        self.order.token = self.after
+
     def finish(self):
         sums = apply_last(
             self.order, self.offsets, self.before, self.two, self.after, self.coupling, self.wave, self.residual, self.norm
         )
-        spans = total_span(sums)
-        self.order.token = spans
-        self.second = total_mode(spans)
+        self.second = total_mode(total_span(sums))
 
     def combine(self):
         sent = combine(self.order, self.amount, self.one, self.two, self.first, self.second, self.peers)
@@ -591,9 +598,10 @@
     ("rest", 0),
     ("gate_high", 1),
     ("again", 0),
-    ("finish", 0),
+    ("settle", 0),
     ("gate_low", 1),
     ("begin", 1),
+    ("finish", 0),
     ("apply", 1),
     ("rest", 1),
     ("combine", 0),
@@ -615,8 +623,10 @@
         setattr(chunk, "low" if part else "high", value)
     for step, which in PLAN:
         getattr(chunks[which], step)()
-    place = jnp.concatenate([c.pick.T for c in chunks], axis=0)
-    return spread(order, [c.value for c in chunks], [c.first for c in chunks], [c.second for c in chunks], place)
+    spans = chunks[0].spans
+    groups = min(spans * amount for _, amount in CHUNKS) // 128 or 1
+    place = jnp.concatenate([pick_matrix(spans // groups, *cut).T for cut in CHUNKS], axis=0)
+    return spread(order, [c.value for c in chunks], [c.first for c in chunks], [c.second for c in chunks], place, spans)
 
 
 def solution(mesh):

time: 465 us -> 447 us (0.961)
  waiting for transfers between devices: 253 us -> 239 us
  local copies, waits for them, and re-layouts: 47.1 us -> 53.5 us
  Pallas kernels: 82.9 us -> 77.4 us
    ppermute x8, waiting for transfers between devices: 132 us -> 94.7 us  [edges(): return (lax.ppermute(last, 'sx', up), lax.ppermute(first, 'sx', down))]
    all_to_all x6, waiting for transfers between devices: 86.3 us -> 98.5 us  [swap(): return lax.all_to_all(value, 'sz', split_axis=0, concat_axis=0, tiled=True)]
    ppermute x24, waiting for transfers between devices: 34.7 us -> 45.7 us  [exchange(): lax.ppermute(value, axis, [(i, i ^ distance) for i in range(lax.axis_size...]
    unnamed x78 -> x80, local copies, waits for them, and re-layouts: 47 us -> 53.3 us
    pallas_call x15, Pallas kernels: 81.7 us -> 76.2 us  [run(): *given, order.token = kernel(*args, order.token)]
where the time goes in v3:
time: 447 us; the launch traced here: 445 us
  waiting for transfers between devices  239 us (53%)
  Pallas kernels  77.4 us (17%)
  starting transfers between devices  65.2 us (15%)
  local copies, waits for them, and re-layouts  53.5 us (12%)
  other arithmetic  9.94 us (2%)
    all_to_all x6, waiting for transfers between devices, swap(): return lax.all_to_all(value, 'sz', split_axis=0, concat_axis=0, tiled=True)  98.5 us
    ppermute x8, waiting for transfers between devices, edges(): return (lax.ppermute(last, 'sx', up), lax.ppermute(first, 'sx', down))  94.7 us
    pallas_call x15, Pallas kernels, run(): *given, order.token = kernel(*args, order.token)  76.2 us
    unnamed x80, local copies, waits for them, and re-layouts  53.3 us
    ppermute x24, waiting for transfers between devices, exchange(): lax.ppermute(value, axis, [(i, i ^ distance) for i in range(lax.axis_size...  45.7 us
    all_to_all x6, starting transfers between devices, swap(): return lax.all_to_all(value, 'sz', split_axis=0, concat_axis=0, tiled=True)  27.4 us
    ppermute x24, starting transfers between devices, exchange(): lax.ppermute(value, axis, [(i, i ^ distance) for i in range(lax.axis_size...  25.9 us
    ppermute x8, starting transfers between devices, edges(): return (lax.ppermute(last, 'sx', up), lax.ppermute(first, 'sx', down))  11.9 us
  transfers between devices with their start and end apart: 38, of which 28 were waited for; matrix products, arithmetic and copies ran while one was open for 2% of the time, Pallas kernels for 14%

profile of v3, /device:TPU:0, one launch (start us, length us, event | category | flops | bytes accessed | tf_op | source)
XLA Modules:
  0.0 445.3 jit_solution(15496526991966993408)
XLA Ops:
  7.6 6.3 %all-to-all-start = ((bf16[8,18,32,256]{3,2,1,0:T(8,128)(2,1)}), bf16[8,18,32,256]{3,2,1,0:T(8,128)(2,1)S(1)}, u32[]{:S(2)}, u32[]{:S(2)}) async-start(bf16[8,18,32,256]{3,2,1,0:T(8,128)(2,1)} %copy-done.28), calls=%async_computation | async-start | bytes 4718592 | tf_op jit(solution)/shard_map/all_to_all | solution.py:501
  17.6 10.3 %shard_map.65 = (s16[8,18,32,256]{3,2,1,0:T(8,128)(2,1)S(1)}, bf16[8,18,32,256]{3,2,1,0:T(8,128)(2,1)S(1)}, s16[8,18,32,256]{3,2,1,0:T(8,128)(2,1)S(1)}, f32[8,128]{1,0:T(8,128)S(1)}) custom-call(f32[18,32,4096]{2,1,0:T(8,128)S(1)} %copy-done.13, bf16[512,256]{1,0:T(8,128)(2,1)S(1)} %get-tuple-element.101.refs_1_, ...), custom_call_target="tpu_custom_call" | custom-call | flops 6039797760 | bytes 16515072 | tf_op jit(solution)/shard_map/pallas_call | solution.py:52
  32.3 36.3 %all-to-all-done.refs_0_.refs_6_.refs_1_ = bf16[8,18,32,256]{3,2,1,0:T(8,128)(2,1)S(1)} async-done(((bf16[8,18,32,256]{3,2,1,0:T(8,128)(2,1)}), bf16[8,18,32,256]{3,2,1,0:T(8,128)(2,1)S(1)}, u32[]{:S(2)}, u32[]{:S(2)}) %all-to-all-start) | async-done | bytes 2359328 | tf_op jit(solution)/shard_map/all_to_all | solution.py:501
  68.6 4.5 %all-to-all-start.1 = ((s16[8,18,32,256]{3,2,1,0:T(8,128)(2,1)}), s16[8,18,32,256]{3,2,1,0:T(8,128)(2,1)}, u32[]{:S(2)}, u32[]{:S(2)}) async-start(s16[8,18,32,256]{3,2,1,0:T(8,128)(2,1)} %copy-done.27), calls=%async_computation.1 | async-start | bytes 4718592 | tf_op jit(solution)/shard_map/all_to_all | solution.py:501
  73.4 4.4 shard_map.66
  80.8 18.3 %collective-permute-done.refs_1_ = bf16[6,256,256]{2,1,0:T(8,128)(2,1)S(1)} collective-permute-done((bf16[6,256,256]{2,1,0:T(8,128)(2,1)S(1)}, bf16[6,256,256]{2,1,0:T(8,128)(2,1)S(1)}, u32[]{:S(2)}, u32[]{:S(2)}) %collective-permute-start) | collective-permute-done | bytes 786464 | tf_op jit(solution)/shard_map/ppermute | solution.py:508
  99.1 16.3 %collective-permute-done.1.refs_3_ = bf16[6,256,256]{2,1,0:T(8,128)(2,1)S(1)} collective-permute-done((bf16[6,256,256]{2,1,0:T(8,128)(2,1)S(1)}, bf16[6,256,256]{2,1,0:T(8,128)(2,1)S(1)}, u32[]{:S(2)}, u32[]{:S(2)}) %collective-permute-start.1) | collective-permute-done | bytes 786464 | tf_op jit(solution)/shard_map/ppermute | solution.py:508
  115.5 4.4 copy-done
  119.8 5.5 %shard_map.67 = (f32[18,256,256]{2,1,0:T(8,128)S(1)}, f32[8,256]{1,0:T(8,128)S(1)}, f32[8,128]{1,0:T(8,128)S(1)}) custom-call(s32[5]{0:T(128)S(1)} %copy-done.34, bf16[6,256,256]{2,1,0:T(8,128)(2,1)S(1)} %collective-permute-done.refs_1_, bf16[18,256,256]{2,1,0:T(8,128)(2,1)S(1)} %get-tuple-element.56.refs_2_.refs_0_, ...), custom_call_target="tpu_custom_call" | custom-call | flops 3019898880 | bytes 23592960 | tf_op jit(solution)/shard_map/pallas_call | solution.py:52
  131.3 4.6 %shard_map.68 = (f32[8,256]{1,0:T(8,128)S(1)}, f32[8,128]{1,0:T(8,128)}) custom-call(f32[18,256,256]{2,1,0:T(8,128)S(1)} %copy-done.9, bf16[8,18,32,256]{3,2,1,0:T(8,128)(2,1)S(1)} %all-to-all-done.refs_0_.refs_6_.refs_1_, s16[8,18,32,256]{3,2,1,0:T(8,128)(2,1)} %all-to-all-done.1.refs_2_.refs_1_, f32[8,256]{1,0:T(8,128)S(1)} %get-tuple-element.62.refs_3_, ...), custom_call_target="tpu_custom_call" | custom-call | flops 2359296 | bytes 9437184 | tf_op jit(solution)/shard_map/pallas_call | solution.py:52
  161.5 7.3 %shard_map.70 = (f32[18,256,256]{2,1,0:T(8,128)S(1)}, bf16[18,256,256]{2,1,0:T(8,128)(2,1)S(1)}, bf16[6,256,256]{2,1,0:T(8,128)(2,1)S(1)}, bf16[6,256,256]{2,1,0...) custom-call(bf16[8,18,32,256]{3,2,1,0:T(8,128)(2,1)S(1)} %copy-done.4, ...), custom_call_target="tpu_custom_call" | custom-call | flops 1207959552 | bytes 16515072 | tf_op jit(solution)/shard_map/pallas_call | solution.py:52
  174.7 16.3 %collective-permute-done.9.token_ref.refs_3_ = bf16[6,256,256]{2,1,0:T(8,128)(2,1)S(1)} collective-permute-done((bf16[6,256,256]{2,1,0:T(8,128)(2,1)S(1)}, bf16[6,256,256]{2,1,0:T(8,128)(2,1)S(1)}, u32[]{:S(2)}, u32[]{:S(2)}) %collective-permute-start.9) | collective-permute-done | bytes 786464 | tf_op jit(solution)/shard_map/ppermute | solution.py:508
  192.5 12.2 %all-to-all-done.2.refs_0_.refs_6_.refs_1_ = bf16[8,18,32,256]{3,2,1,0:T(8,128)(2,1)S(1)} async-done(((bf16[8,18,32,256]{3,2,1,0:T(8,128)(2,1)}), bf16[8,18,32,256]{3,2,1,0:T(8,128)(2,1)S(1)}, u32[]{:S(2)}, u32[]{:S(2)}) %all-to-all-start.2) | async-done | bytes 2359328 | tf_op jit(solution)/shard_map/all_to_all | solution.py:501
  204.7 4.5 %all-to-all-start.3 = ((s16[8,18,32,256]{3,2,1,0:T(8,128)(2,1)}), s16[8,18,32,256]{3,2,1,0:T(8,128)(2,1)}, u32[]{:S(2)}, u32[]{:S(2)}) async-start(s16[8,18,32,256]{3,2,1,0:T(8,128)(2,1)} %get-tuple-element.83), calls=%async_computation.3 | async-start | bytes 4718592 | tf_op jit(solution)/shard_map/all_to_all | solution.py:501
  211.6 4.3 shard_map.72
  219.0 11.7 %collective-permute-done.8.refs_1_ = bf16[6,256,256]{2,1,0:T(8,128)(2,1)S(1)} collective-permute-done((bf16[6,256,256]{2,1,0:T(8,128)(2,1)}, bf16[6,256,256]{2,1,0:T(8,128)(2,1)S(1)}, u32[]{:S(2)}, u32[]{:S(2)}) %collective-permute-start.8) | collective-permute-done | bytes 786464 | tf_op jit(solution)/shard_map/ppermute | solution.py:508
  230.7 4.4 copy-done.1
  237.4 5.2 %shard_map.73 = (f32[8,256]{1,0:T(8,128)S(1)}, f32[8,128]{1,0:T(8,128)S(1)}) custom-call(s32[5]{0:T(128)S(1)} %copy-done.34, bf16[6,256,256]{2,1,0:T(8,128)(2,1)S(1)} %collective-permute-done.8.refs_1_, bf16[18,256,256]{2,1,0:T(8,128)(2,1)S(1)} %copy-done.19, bf16[6,256,256]{2,1,0:T(8,128)(2,1)S(1)} %copy-done.26, bf16[18,5,256,256]{3,2,1,0:T(8,128)(2,1)S(1)} %copy-done.1, ...), custom_call_target="tpu_custom_call" | custom-call | flops 3019898880 | bytes 18874368 | tf_op jit(solution)/shard_map/pallas_call | solution.py:52
  248.3 4.2 collective-permute-done.13
  252.5 12.0 %collective-permute-done.12 = f32[8,256]{1,0:T(8,128)S(1)} collective-permute-done((f32[8,256]{1,0:T(8,128)S(1)}, f32[8,256]{1,0:T(8,128)S(1)}, u32[]{:S(2)}, u32[]{:S(2)}) %collective-permute-start.12) | collective-permute-done | bytes 8224 | tf_op jit(solution)/shard_map/ppermute | solution.py:512
  266.0 5.5 %shard_map.74 = (f32[18,256,256]{2,1,0:T(8,128)S(1)}, f32[8,256]{1,0:T(8,128)S(1)}, f32[8,128]{1,0:T(8,128)S(1)}) custom-call(s32[5]{0:T(128)S(1)} %copy-done.34, bf16[6,256,256]{2,1,0:T(8,128)(2,1)S(1)} %collective-permute-done.16.refs_1_, bf16[18,256,256]{2,1,0:T(8,128)(2,1)S(1)} %get-tuple-element.79.refs_2_.refs_0_, ...), custom_call_target="tpu_custom_call" | custom-call | flops 3019898880 | bytes 23592960 | tf_op jit(solution)/shard_map/pallas_call | solution.py:52
  276.1 5.0 %shard_map.75 = (f32[8,256]{1,0:T(8,128)S(1)}, f32[8,128]{1,0:T(8,128)}) custom-call(f32[18,256,256]{2,1,0:T(8,128)S(1)} %copy-done.6, bf16[8,18,32,256]{3,2,1,0:T(8,128)(2,1)S(1)} %all-to-all-done.2.refs_0_.refs_6_.refs_1_, s16[8,18,32,256]{3,2,1,0:T(8,128)(2,1)} %all-to-all-done.3.refs_2_.refs_1_, f32[8,256]{1,0:T(8,128)S(1)} %get-tuple-element.84.refs_3_, ...), custom_call_target="tpu_custom_call" | custom-call | flops 2359296 | bytes 9437184 | tf_op jit(solution)/shard_map/pallas_call | solution.py:52
  291.8 4.7 %all-to-all-start.4 = ((f16[8,18,32,256]{3,2,1,0:T(8,128)(2,1)}), f16[8,18,32,256]{3,2,1,0:T(8,128)(2,1)}, u32[]{:S(2)}, u32[]{:S(2)}) async-start(f16[8,18,32,256]{3,2,1,0:T(8,128)(2,1)} %convert_element_type.46), calls=%async_computation.4 | async-start | bytes 4718592 | tf_op jit(solution)/shard_map/all_to_all | solution.py:501
  306.2 6.7 %shard_map.77 = (f32[18,256,256]{2,1,0:T(8,128)S(1)}, bf16[18,256,256]{2,1,0:T(8,128)(2,1)S(1)}, bf16[6,256,256]{2,1,0:T(8,128)(2,1)S(1)}, bf16[6,256,256]{2,1,0...) custom-call(bf16[8,18,32,256]{3,2,1,0:T(8,128)(2,1)S(1)} %all-to-all-done.2.refs_0_.refs_6_.refs_1_, ...), custom_call_target="tpu_custom_call" | custom-call | flops 1207959552 | bytes 16515072 | tf_op jit(solution)/shard_map/pallas_call | solution.py:52
  315.9 18.5 %collective-permute-done.24.refs_1_ = bf16[6,256,256]{2,1,0:T(8,128)(2,1)S(1)} collective-permute-done((bf16[6,256,256]{2,1,0:T(8,128)(2,1)S(1)}, bf16[6,256,256]{2,1,0:T(8,128)(2,1)S(1)}, u32[]{:S(2)}, u32[]{:S(2)}) %collective-permute-start.24) | collective-permute-done | bytes 786464 | tf_op jit(solution)/shard_map/ppermute | solution.py:508
  334.3 13.5 %collective-permute-done.25.refs_3_ = bf16[6,256,256]{2,1,0:T(8,128)(2,1)S(1)} collective-permute-done((bf16[6,256,256]{2,1,0:T(8,128)(2,1)S(1)}, bf16[6,256,256]{2,1,0:T(8,128)(2,1)S(1)}, u32[]{:S(2)}, u32[]{:S(2)}) %collective-permute-start.25) | collective-permute-done | bytes 786464 | tf_op jit(solution)/shard_map/ppermute | solution.py:508
  347.9 4.3 copy-done.2
  352.2 5.2 %shard_map.78 = (f32[8,256]{1,0:T(8,128)S(1)}, f32[8,128]{1,0:T(8,128)S(1)}) custom-call(s32[5]{0:T(128)S(1)} %copy-done.34, bf16[6,256,256]{2,1,0:T(8,128)(2,1)S(1)} %collective-permute-done.24.refs_1_, bf16[18,256,256]{2,1,0:T(8,128)(2,1)S(1)} %get-tuple-element.90.refs_2_.refs_1_, bf16[6,256,256]{2,1,0:T(8,128)(2,1)S(1)} %collective-permute-done.25.refs_3_, ...), custom_call_target="tpu_custom_call" | custom-call | flops 3019898880 | bytes 18874368 | tf_op jit(solution)/shard_map/pallas_call | solution.py:52
  358.7 3.9 collective-permute-start.29
  381.9 4.4 convert_element_type.47.refs_0_
  386.3 50.0 %all-to-all-done.5 = f16[8,18,32,256]{3,2,1,0:T(8,128)(2,1)S(1)} async-done(((f16[8,18,32,256]{3,2,1,0:T(8,128)(2,1)}), f16[8,18,32,256]{3,2,1,0:T(8,128)(2,1)S(1)}, u32[]{:S(2)}, u32[]{:S(2)}) %all-to-all-start.5) | async-done | bytes 2359328 | tf_op jit(solution)/shard_map/all_to_all | solution.py:501
  438.7 6.7 %shard_map.80 = (f32[18,32,4096]{2,1,0:T(8,128)}, f32[8,128]{1,0:T(8,128)}) custom-call(f32[8,18,32,256]{3,2,1,0:T(8,128)S(1)} %copy-done.11, f32[8,18,32,256]{3,2,1,0:T(8,128)S(1)} %convert_element_type.49.refs_1_, f32[8,256]{1,0:T(8,128)S(1)} %add.271.refs_3_.refs_2_, f32[8,256]{1,0:T(8,128)S(1)} %add.283.refs_3_.refs_2_, ...), custom_call_target="tpu_custom_call" | custom-call | flops 2415919104 | bytes 18874368 | tf_op jit(solution)/shard_map/pallas_call | solution.py:52
  (173 shorter events, 123.4 us)
Async XLA Ops:
  7.6 61.0 %all-to-all-start = ((bf16[8,18,32,256]{3,2,1,0:T(8,128)(2,1)}), bf16[8,18,32,256]{3,2,1,0:T(8,128)(2,1)S(1)}, u32[]{:S(2)}, u32[]{:S(2)}) async-start(bf16[8,18,32,256]{3,2,1,0:T(8,128)(2,1)} %copy-done.28), calls=%async_computation | async-start | bytes 4718592 | tf_op jit(solution)/shard_map/all_to_all | solution.py:501
  68.6 60.3 %all-to-all-start.1 = ((s16[8,18,32,256]{3,2,1,0:T(8,128)(2,1)}), s16[8,18,32,256]{3,2,1,0:T(8,128)(2,1)}, u32[]{:S(2)}, u32[]{:S(2)}) async-start(s16[8,18,32,256]{3,2,1,0:T(8,128)(2,1)} %copy-done.27), calls=%async_computation.1 | async-start | bytes 4718592 | tf_op jit(solution)/shard_map/all_to_all | solution.py:501
  77.8 21.3 %collective-permute-start = (bf16[6,256,256]{2,1,0:T(8,128)(2,1)S(1)}, bf16[6,256,256]{2,1,0:T(8,128)(2,1)S(1)}, u32[]{:S(2)}, u32[]{:S(2)}) collective-permute-start(bf16[6,256,256]{2,1,0:T(8,128)(2,1)S(1)} %get-tuple-element.58), channel_id=1, source_target_pairs={{0,8},{8,16},{16,24},{24,0},{1,9},{9,17},{17,25},{25,1},{2,10},{10... | collective-permute-start | bytes 2359304 | tf_op jit(solution)/shard_map/ppermute | solution.py:508
  79.4 36.1 %collective-permute-start.1 = (bf16[6,256,256]{2,1,0:T(8,128)(2,1)S(1)}, bf16[6,256,256]{2,1,0:T(8,128)(2,1)S(1)}, u32[]{:S(2)}, u32[]{:S(2)}) collective-permute-start(bf16[6,256,256]{2,1,0:T(8,128)(2,1)S(1)} %get-tuple-element.59), channel_id=1, source_target_pairs={{8,0},{16,8},{24,16},{0,24},{9,1},{17,9},{25,17},{1,25},{10,2},{18... | collective-permute-start | bytes 2359304 | tf_op jit(solution)/shard_map/ppermute | solution.py:508
  137.0 5.4 %collective-permute-start.5 = (f32[8,256]{1,0:T(8,128)S(1)}, f32[8,256]{1,0:T(8,128)S(1)}, u32[]{:S(2)}, u32[]{:S(2)}) collective-permute-start(f32[8,256]{1,0:T(8,128)S(1)} %add.266), channel_id=1, source_target_pairs={{0,6},{1,7},{2,4},{3,5},{4,2},{5,3},{6,0},{7,1},{8,14},{9,15},{10,... | collective-permute-start | bytes 24584 | tf_op jit(solution)/shard_map/ppermute | solution.py:512
  140.6 4.5 %collective-permute-start.4 = (f32[8,256]{1,0:T(8,128)S(1)}, f32[8,256]{1,0:T(8,128)S(1)}, u32[]{:S(2)}, u32[]{:S(2)}) collective-permute-start(f32[8,256]{1,0:T(8,128)S(1)} %add.266), channel_id=1, source_target_pairs={{0,4},{1,5},{2,6},{3,7},{4,0},{5,1},{6,2},{7,3},{8,12},{9,13},{10,... | collective-permute-start | bytes 24584 | tf_op jit(solution)/shard_map/ppermute | solution.py:512
  140.6 4.5 %collective-permute-start.3 = (f32[8,256]{1,0:T(8,128)S(1)}, f32[8,256]{1,0:T(8,128)S(1)}, u32[]{:S(2)}, u32[]{:S(2)}) collective-permute-start(f32[8,256]{1,0:T(8,128)S(1)} %add.266), channel_id=1, source_target_pairs={{0,2},{1,3},{2,0},{3,1},{4,6},{5,7},{6,4},{7,5},{8,10},{9,11},{10,... | collective-permute-start | bytes 24584 | tf_op jit(solution)/shard_map/ppermute | solution.py:512
  146.3 58.4 %all-to-all-start.2 = ((bf16[8,18,32,256]{3,2,1,0:T(8,128)(2,1)}), bf16[8,18,32,256]{3,2,1,0:T(8,128)(2,1)S(1)}, u32[]{:S(2)}, u32[]{:S(2)}) async-start(bf16[8,18,32,256]{3,2,1,0:T(8,128)(2,1)} %get-tuple-element.73), calls=%async_computation.2 | async-start | bytes 4718592 | tf_op jit(solution)/shard_map/all_to_all | solution.py:501
  150.1 3.7 collective-permute-start.6
  173.2 17.8 %collective-permute-start.9 = (bf16[6,256,256]{2,1,0:T(8,128)(2,1)S(1)}, bf16[6,256,256]{2,1,0:T(8,128)(2,1)S(1)}, u32[]{:S(2)}, u32[]{:S(2)}) collective-permute-start(bf16[6,256,256]{2,1,0:T(8,128)(2,1)S(1)} %get-tuple-element.70), channel_id=1, source_target_pairs={{8,0},{16,8},{24,16},{0,24},{9,1},{17,9},{25,17},{1,25},{10,2},{18... | collective-permute-start | bytes 2359304 | tf_op jit(solution)/shard_map/ppermute | solution.py:508
  204.7 69.1 %all-to-all-start.3 = ((s16[8,18,32,256]{3,2,1,0:T(8,128)(2,1)}), s16[8,18,32,256]{3,2,1,0:T(8,128)(2,1)}, u32[]{:S(2)}, u32[]{:S(2)}) async-start(s16[8,18,32,256]{3,2,1,0:T(8,128)(2,1)} %get-tuple-element.83), calls=%async_computation.3 | async-start | bytes 4718592 | tf_op jit(solution)/shard_map/all_to_all | solution.py:501
  209.2 21.5 %collective-permute-start.8 = (bf16[6,256,256]{2,1,0:T(8,128)(2,1)}, bf16[6,256,256]{2,1,0:T(8,128)(2,1)S(1)}, u32[]{:S(2)}, u32[]{:S(2)}) collective-permute-start(bf16[6,256,256]{2,1,0:T(8,128)(2,1)} %copy-done.36), channel_id=1, source_target_pairs={{0,8},{8,16},{16,24},{24,0},{1,9},{9,17},{17,25},{25,1},{2,10},{10... | collective-permute-start | bytes 2359304 | tf_op jit(solution)/shard_map/ppermute | solution.py:508
  216.0 50.0 %collective-permute-start.16 = (bf16[6,256,256]{2,1,0:T(8,128)(2,1)S(1)}, bf16[6,256,256]{2,1,0:T(8,128)(2,1)S(1)}, u32[]{:S(2)}, u32[]{:S(2)}) collective-permute-start(bf16[6,256,256]{2,1,0:T(8,128)(2,1)S(1)} %get-tuple-element.78), channel_id=1, source_target_pairs={{0,8},{8,16},{16,24},{24,0},{1,9},{9,17},{17,25},{25,1},{2,10},{10... | collective-permute-start | bytes 2359304 | tf_op jit(solution)/shard_map/ppermute | solution.py:508
  216.8 49.2 %collective-permute-start.17 = (bf16[6,256,256]{2,1,0:T(8,128)(2,1)S(1)}, bf16[6,256,256]{2,1,0:T(8,128)(2,1)S(1)}, u32[]{:S(2)}, u32[]{:S(2)}) collective-permute-start(bf16[6,256,256]{2,1,0:T(8,128)(2,1)S(1)} %get-tuple-element.80), channel_id=1, source_target_pairs={{8,0},{16,8},{24,16},{0,24},{9,1},{17,9},{25,17},{1,25},{10,2},{18... | collective-permute-start | bytes 2359304 | tf_op jit(solution)/shard_map/ppermute | solution.py:508
  243.9 8.6 %collective-permute-start.13 = (f32[8,256]{1,0:T(8,128)S(1)}, f32[8,256]{1,0:T(8,128)S(1)}, u32[]{:S(2)}, u32[]{:S(2)}) collective-permute-start(f32[8,256]{1,0:T(8,128)S(1)} %add.272), channel_id=1, source_target_pairs={{0,6},{1,7},{2,4},{3,5},{4,2},{5,3},{6,0},{7,1},{8,14},{9,15},{10,... | collective-permute-start | bytes 24584 | tf_op jit(solution)/shard_map/ppermute | solution.py:512
  247.6 16.9 %collective-permute-start.12 = (f32[8,256]{1,0:T(8,128)S(1)}, f32[8,256]{1,0:T(8,128)S(1)}, u32[]{:S(2)}, u32[]{:S(2)}) collective-permute-start(f32[8,256]{1,0:T(8,128)S(1)} %add.272), channel_id=1, source_target_pairs={{0,4},{1,5},{2,6},{3,7},{4,0},{5,1},{6,2},{7,3},{8,12},{9,13},{10,... | collective-permute-start | bytes 24584 | tf_op jit(solution)/shard_map/ppermute | solution.py:512
  247.6 16.9 %collective-permute-start.11 = (f32[8,256]{1,0:T(8,128)S(1)}, f32[8,256]{1,0:T(8,128)S(1)}, u32[]{:S(2)}, u32[]{:S(2)}) collective-permute-start(f32[8,256]{1,0:T(8,128)S(1)} %add.272), channel_id=1, source_target_pairs={{0,2},{1,3},{2,0},{3,1},{4,6},{5,7},{6,4},{7,5},{8,10},{9,11},{10,... | collective-permute-start | bytes 24584 | tf_op jit(solution)/shard_map/ppermute | solution.py:512
  264.5 16.6 %collective-permute-start.14 = (f32[8,256]{1,0:T(8,128)S(1)}, f32[8,256]{1,0:T(8,128)S(1)}, u32[]{:S(2)}, u32[]{:S(2)}) collective-permute-start(f32[8,256]{1,0:T(8,128)S(1)} %add_add_fusion.2), channel_id=1, source_target_pairs={{0,8},{8,0},{16,24},{24,16},{1,9},{9,1},{17,25},{25,17},{2,10},{10... | collective-permute-start | bytes 24584 | tf_op jit(solution)/shard_map/ppermute | solution.py:512
  281.1 5.6 %collective-permute-start.15 = (f32[8,256]{1,0:T(8,128)S(1)}, f32[8,256]{1,0:T(8,128)S(1)}, u32[]{:S(2)}, u32[]{:S(2)}) collective-permute-start(f32[8,256]{1,0:T(8,128)S(1)} %add.276), channel_id=1, source_target_pairs={{0,16},{8,24},{16,0},{24,8},{1,17},{9,25},{17,1},{25,9},{2,18},{10... | collective-permute-start | bytes 24584 | tf_op jit(solution)/shard_map/ppermute | solution.py:512
  282.2 5.4 %collective-permute-start.21 = (f32[8,256]{1,0:T(8,128)S(1)}, f32[8,256]{1,0:T(8,128)S(1)}, u32[]{:S(2)}, u32[]{:S(2)}) collective-permute-start(f32[8,256]{1,0:T(8,128)S(1)} %add.278), channel_id=1, source_target_pairs={{0,6},{1,7},{2,4},{3,5},{4,2},{5,3},{6,0},{7,1},{8,14},{9,15},{10,... | collective-permute-start | bytes 24584 | tf_op jit(solution)/shard_map/ppermute | solution.py:512
  283.5 4.5 %collective-permute-start.20 = (f32[8,256]{1,0:T(8,128)S(1)}, f32[8,256]{1,0:T(8,128)S(1)}, u32[]{:S(2)}, u32[]{:S(2)}) collective-permute-start(f32[8,256]{1,0:T(8,128)S(1)} %add.278), channel_id=1, source_target_pairs={{0,4},{1,5},{2,6},{3,7},{4,0},{5,1},{6,2},{7,3},{8,12},{9,13},{10,... | collective-permute-start | bytes 24584 | tf_op jit(solution)/shard_map/ppermute | solution.py:512
  284.2 4.1 collective-permute-start.19
  291.8 86.3 %all-to-all-start.4 = ((f16[8,18,32,256]{3,2,1,0:T(8,128)(2,1)}), f16[8,18,32,256]{3,2,1,0:T(8,128)(2,1)}, u32[]{:S(2)}, u32[]{:S(2)}) async-start(f16[8,18,32,256]{3,2,1,0:T(8,128)(2,1)} %convert_element_type.46), calls=%async_computation.4 | async-start | bytes 4718592 | tf_op jit(solution)/shard_map/all_to_all | solution.py:501
  296.5 3.7 collective-permute-start.22
  300.2 3.7 collective-permute-start.23
  312.9 21.4 %collective-permute-start.24 = (bf16[6,256,256]{2,1,0:T(8,128)(2,1)S(1)}, bf16[6,256,256]{2,1,0:T(8,128)(2,1)S(1)}, u32[]{:S(2)}, u32[]{:S(2)}) collective-permute-start(bf16[6,256,256]{2,1,0:T(8,128)(2,1)S(1)} %get-tuple-element.91), channel_id=1, source_target_pairs={{0,8},{8,16},{16,24},{24,0},{1,9},{9,17},{17,25},{25,1},{2,10},{10... | collective-permute-start | bytes 2359304 | tf_op jit(solution)/shard_map/ppermute | solution.py:508
  313.8 34.1 %collective-permute-start.25 = (bf16[6,256,256]{2,1,0:T(8,128)(2,1)S(1)}, bf16[6,256,256]{2,1,0:T(8,128)(2,1)S(1)}, u32[]{:S(2)}, u32[]{:S(2)}) collective-permute-start(bf16[6,256,256]{2,1,0:T(8,128)(2,1)S(1)} %get-tuple-element.92), channel_id=1, source_target_pairs={{8,0},{16,8},{24,16},{0,24},{9,1},{17,9},{25,17},{1,25},{10,2},{18... | collective-permute-start | bytes 2359304 | tf_op jit(solution)/shard_map/ppermute | solution.py:508
  358.7 5.5 %collective-permute-start.29 = (f32[8,256]{1,0:T(8,128)S(1)}, f32[8,256]{1,0:T(8,128)S(1)}, u32[]{:S(2)}, u32[]{:S(2)}) collective-permute-start(f32[8,256]{1,0:T(8,128)S(1)} %add.284), channel_id=1, source_target_pairs={{0,6},{1,7},{2,4},{3,5},{4,2},{5,3},{6,0},{7,1},{8,14},{9,15},{10,... | collective-permute-start | bytes 24584 | tf_op jit(solution)/shard_map/ppermute | solution.py:512
  362.6 4.5 %collective-permute-start.28 = (f32[8,256]{1,0:T(8,128)S(1)}, f32[8,256]{1,0:T(8,128)S(1)}, u32[]{:S(2)}, u32[]{:S(2)}) collective-permute-start(f32[8,256]{1,0:T(8,128)S(1)} %add.284), channel_id=1, source_target_pairs={{0,4},{1,5},{2,6},{3,7},{4,0},{5,1},{6,2},{7,3},{8,12},{9,13},{10,... | collective-permute-start | bytes 24584 | tf_op jit(solution)/shard_map/ppermute | solution.py:512
  362.6 4.5 %collective-permute-start.27 = (f32[8,256]{1,0:T(8,128)S(1)}, f32[8,256]{1,0:T(8,128)S(1)}, u32[]{:S(2)}, u32[]{:S(2)}) collective-permute-start(f32[8,256]{1,0:T(8,128)S(1)} %add.284), channel_id=1, source_target_pairs={{0,2},{1,3},{2,0},{3,1},{4,6},{5,7},{6,4},{7,5},{8,10},{9,11},{10,... | collective-permute-start | bytes 24584 | tf_op jit(solution)/shard_map/ppermute | solution.py:512
  367.1 3.7 collective-permute-start.30
  378.1 58.2 %all-to-all-start.5 = ((f16[8,18,32,256]{3,2,1,0:T(8,128)(2,1)}), f16[8,18,32,256]{3,2,1,0:T(8,128)(2,1)S(1)}, u32[]{:S(2)}, u32[]{:S(2)}) async-start(f16[8,18,32,256]{3,2,1,0:T(8,128)(2,1)} %convert_element_type.48), calls=%async_computation.5 | async-start | bytes 4718592 | tf_op jit(solution)/shard_map/all_to_all | solution.py:501
  (46 other events, 366.8 us)
